TPU v7x, 256 devices: a whole 4x4x8 slice. The times are simulated.
256 devices in a mesh: tm: 32 (over y, z_lo, core), rows: 8 (over x, z_hi).
Axes of the slice: x: 4, y: 4, z: 8 (z_hi: 2, z_lo: 4; z = z_hi * 4 + z_lo), core: 2. Of those that a mesh axis runs over, the one named last changes fastest.
Arguments:
- noisy_states: float32 [128, 2, 64, 256], P('tm', None, 'rows'), may hold values from -6 to 6
- noise_first: float32 [128, 2, 64, 256], P('tm', None, 'rows'), may hold values from -6 to 6
- noise_second: float32 [128, 2, 64, 256], P('tm', None, 'rows'), may hold values from -6 to 6
- conv_in: bfloat16 [9, 96, 18], replicated, may hold values from -0.5 to 0.5
- conv_out: bfloat16 [9, 2, 96], replicated, may hold values from -0.21875 to 0.21875
- level_embed: float32 [96], replicated, may hold values from -4 to 4
- obs_count: int32 [32, 8], P('tm', 'rows'), may hold values from 1 to 256, as said below
- obs_step: int32 [32, 8, 256], P('tm', 'rows'), may hold values from 0 to 3
- obs_row: int32 [32, 8, 256], P('tm', 'rows'), may hold values from 0 to 7
- obs_col: int32 [32, 8, 256], P('tm', 'rows'), may hold values from 0 to 255
- obs_value: float32 [32, 8, 256], P('tm', 'rows'), may hold values from -4 to 4
Outputs:
- final_states: float32 [128, 2, 64, 256], P('tm', None, 'rows')
Inputs may be any that keep to these rules, and one draw needn't show every extreme that they name: `obs_count`: some block has exactly 256 live observations in every draw; the counts are skewed over blocks.
All inputs are finite; a program needn't handle non-finite values.
Results may differ from a plain program's by a relative error of at most 0.0014.
Values may be sent and summed in bfloat16 or wider, within the bound.
A program may use at most 64 MiB of HBM per device.

v0:
```python
import jax
import jax.numpy as jnp
from jax import lax
from jax.sharding import PartitionSpec as P

K = 4


LEVELS = (1.0, 0.5, 0.2)
OBS_NOISE = 0.1
COVARIANCE_GAIN = 0.5


def with_halo(cells, sides, width, closed):
    for axis, dim in sides:
        count = lax.axis_size(axis)
        ends = count if closed else count - 1
        head = lax.slice_in_dim(cells, 0, width, axis=dim)
        tail = lax.slice_in_dim(cells, cells.shape[dim] - width, cells.shape[dim], axis=dim)
        cells = jnp.concatenate(
            [
                lax.ppermute(tail, axis, [(i, (i + 1) % count) for i in range(ends)]),
                cells,
                lax.ppermute(head, axis, [((i + 1) % count, i) for i in range(ends)]),
            ],
            axis=dim,
        )
    return cells


def conv_three(window, weights, out_rows):
    summed = jnp.zeros((weights.shape[1], out_rows, window.shape[2]), jnp.float32)
    for row_off in range(3):
        for col_off in range(3):
            shifted = jnp.roll(window[:, row_off : row_off + out_rows, :], 1 - col_off, axis=2)
            summed = summed + jnp.einsum(
                "oc,crw->orw",
                weights[3 * row_off + col_off],
                shifted,
                preferred_element_type=jnp.float32,
            )
    return summed


def denoise_net(scaled, conv_in, conv_out, level_embed, level_now):
    frames_here, layer_count, rows_here, columns = scaled.shape
    rim_width = 1
    framed = with_halo(scaled, (("tm", 0),), K, False)
    padded = with_halo(framed, (("rows", 2),), rim_width, True)
    hidden_rows = rows_here + 2 * (rim_width - 1)
    channels = layer_count * (2 * K + 1)

    def hidden_at(position):
        window = lax.dynamic_slice_in_dim(padded, position, 2 * K + 1, 0).reshape(
            channels, rows_here + 2 * rim_width, columns
        )
        summed = conv_three(window, conv_in, hidden_rows) + level_now * level_embed[:, None, None]
        return jax.nn.silu(summed).astype(jnp.bfloat16)

    hidden = lax.map(hidden_at, jnp.arange(frames_here, dtype=jnp.int32))
    hidden = with_halo(hidden, (("rows", 2),), 1, True)

    def output_at(block):
        return conv_three(block, conv_out, rows_here)

    return lax.map(output_at, hidden)


def observe_guide(denoised, level_now, live_count, cell_index, col_index, values):
    frames_here, layer_count, rows_here, columns = denoised.shape
    upper = denoised[:, 0].reshape(frames_here * rows_here, columns)
    slots = cell_index.shape[0]
    active_slot = jnp.arange(slots, dtype=jnp.int32) < live_count
    cells_hot = (
        cell_index[:, None] == jnp.arange(frames_here * rows_here, dtype=jnp.int32)[None, :]
    ).astype(jnp.float32)
    cols_hot = (col_index[:, None] == jnp.arange(columns, dtype=jnp.int32)[None, :]).astype(
        jnp.float32
    )
    picked = jnp.sum(jnp.dot(cells_hot, upper, precision=lax.Precision.HIGHEST) * cols_hot, axis=1)
    misfit = jnp.where(
        active_slot,
        (values - picked) / (OBS_NOISE + COVARIANCE_GAIN * level_now**2),
        jnp.float32(0.0),
    )
    guide_upper = jnp.dot(cells_hot.T, cols_hot * misfit[:, None], precision=lax.Precision.HIGHEST)
    guide_upper = guide_upper.reshape(frames_here, 1, rows_here, columns)
    lower_zero = jnp.zeros((frames_here, layer_count - 1, rows_here, columns), jnp.float32)
    return jnp.concatenate([guide_upper, lower_zero], axis=1)


def per_device(
    noisy_states,
    noise_first,
    noise_second,
    conv_in,
    conv_out,
    level_embed,
    obs_count,
    obs_step,
    obs_row,
    obs_col,
    obs_value,
):
    rows_here = noisy_states.shape[2]
    live_count = obs_count.reshape(-1)[0]
    cell_index = obs_step.reshape(-1) * rows_here + obs_row.reshape(-1)
    col_index = obs_col.reshape(-1)
    values = obs_value.reshape(-1)
    current = noisy_states
    for index_level, noise_draw in enumerate((noise_first, noise_second)):
        level_now = LEVELS[index_level]
        level_next = LEVELS[index_level + 1]
        scaled = (current / jnp.sqrt(1.0 + level_now**2)).astype(jnp.bfloat16)
        net = denoise_net(scaled, conv_in, conv_out, level_embed, level_now)
        denoised = current / (1.0 + level_now**2) + level_now / jnp.sqrt(1.0 + level_now**2) * net
        guide = observe_guide(denoised, level_now, live_count, cell_index, col_index, values)
        score = (denoised - current) / level_now**2 + guide
        spread = level_now**2 - level_next**2
        current = current + spread * score + spread**0.5 * noise_draw
    return current


def solution(mesh):
    in_specs = (
        P("tm", None, "rows", None),
        P("tm", None, "rows", None),
        P("tm", None, "rows", None),
        P(),
        P(),
        P(),
        P("tm", "rows"),
        P("tm", "rows", None),
        P("tm", "rows", None),
        P("tm", "rows", None),
        P("tm", "rows", None),
    )
    out_specs = P("tm", None, "rows", None)
    return jax.shard_map(
        per_device, mesh=mesh, in_specs=in_specs, out_specs=out_specs, check_vma=False
    )
```

profile of v0, /device:TPU:99, one launch (start us, length us, event | category | flops | bytes accessed | tf_op | source)
XLA Modules:
  0.0 165.7 jit_solution(17842282840919426241)
XLA Ops:
  0.0 0.9 multiply_convert_fusion.3
  0.9 2.4 %collective-permute-start = (bf16[4,2,8,256]{3,2,1,0:T(8,128)(2,1)S(1)}, bf16[4,2,8,256]{3,2,1,0:T(8,128)(2,1)S(1)}, u32[]{:S(2)}, u32[]{:S(2)}) collective-permute-start(bf16[4,2,8,256]{3,2,1,0:T(8,128)(2,1)S(1)} %multiply_convert_fusion.3), channel_id=1, source_target_pairs={{0,8},{8,16},{16,24},{24,32},{32,40},{40,48},{48,56},{56,64},{64,7... | collective-permute-start | bytes 98312 | tf_op jit(solution)/shard_map/ppermute | solution.py:22
  3.3 2.1 %collective-permute-start.1 = (bf16[4,2,8,256]{3,2,1,0:T(8,128)(2,1)S(1)}, bf16[4,2,8,256]{3,2,1,0:T(8,128)(2,1)S(1)}, u32[]{:S(2)}, u32[]{:S(2)}) collective-permute-start(bf16[4,2,8,256]{3,2,1,0:T(8,128)(2,1)S(1)} %multiply_convert_fusion.3), channel_id=1, source_target_pairs={{8,0},{16,8},{24,16},{32,24},{40,32},{48,40},{56,48},{64,56},{72,6... | collective-permute-start | bytes 98312 | tf_op jit(solution)/shard_map/ppermute | solution.py:24
  5.4 5.8 %collective-permute-done.1 = bf16[4,2,8,256]{3,2,1,0:T(8,128)(2,1)S(1)} collective-permute-done((bf16[4,2,8,256]{3,2,1,0:T(8,128)(2,1)S(1)}, bf16[4,2,8,256]{3,2,1,0:T(8,128)(2,1)S(1)}, u32[]{:S(2)}, u32[]{:S(2)}) %collective-permute-start.1) | collective-permute-done | bytes 32800 | tf_op jit(solution)/shard_map/ppermute | solution.py:24
  11.2 7.1 %collective-permute-start.2 = (bf16[12,2,1,256]{3,2,1,0:T(2,128)(2,1)S(1)}, bf16[12,2,1,256]{3,2,1,0:T(2,128)(2,1)S(1)}, u32[]{:S(2)}, u32[]{:S(2)}) collective-permute-start(bf16[12,2,1,256]{3,2,1,0:T(2,128)(2,1)S(1)} %get-tuple-element.237), channel_id=1, source_target_pairs={{0,1},{1,2},{2,3},{3,4},{4,5},{5,6},{6,7},{7,0},{8,9},{9,10},{10,1... | collective-permute-start | bytes 36872 | tf_op jit(solution)/shard_map/ppermute | solution.py:22
  19.0 0.6 collective-permute-done.2
  19.6 5.3 %collective-permute-done.3 = bf16[12,2,1,256]{3,2,1,0:T(2,128)(2,1)S(1)} collective-permute-done((bf16[12,2,1,256]{3,2,1,0:T(2,128)(2,1)S(1)}, bf16[12,2,1,256]{3,2,1,0:T(2,128)(2,1)S(1)}, u32[]{:S(2)}, u32[]{:S(2)}) %collective-permute-start.3) | collective-permute-done | bytes 12320 | tf_op jit(solution)/shard_map/ppermute | solution.py:24
  25.4 23.6 %while.40 = (s32[]{:T(128)}, bf16[4,96,8,256]{3,1,2,0:T(8,128)(2,1)S(1)}, s32[4]{0:T(128)S(1)}, bf16[12,2,10,256]{3,1,0,2:T(2,128)(2,1)S(1)}, bf16[9,96,18]{1,2,...) while((s32[]{:T(128)}, bf16[4,96,8,256]{3,1,2,0:T(8,128)(2,1)S(1)}, ...), condition=%wide.region_1.2_spmd, body=%wide.region_0.1_spmd.sunk | while | flops 67338240 | bytes 15538835 | solution.py:60
  25.4 0.6 dynamic_slice.31
  29.2 0.3 fusion.402
  30.2 0.3 fusion.403
  30.8 0.4 fusion.404
  31.3 0.6 dynamic_slice.31
  36.1 0.3 fusion.403
  36.7 0.4 fusion.404
  37.2 0.6 dynamic_slice.31
  41.0 0.3 fusion.402
  42.0 0.3 fusion.403
  42.6 0.4 fusion.404
  43.1 0.6 dynamic_slice.31
  46.9 0.3 fusion.402
  47.9 0.3 fusion.403
  48.5 0.4 fusion.404
  49.0 1.3 collective-permute-start.4
  50.3 5.0 %collective-permute-start.5 = (bf16[4,96,1,256]{3,1,2,0:T(8,128)(2,1)S(1)}, bf16[4,96,1,256]{3,1,2,0:T(8,128)(2,1)S(1)}, u32[]{:S(2)}, u32[]{:S(2)}) collective-permute-start(bf16[4,96,1,256]{3,1,2,0:T(8,128)(2,1)S(1)} %get-tuple-element.234), channel_id=1, source_target_pairs={{1,0},{2,1},{3,2},{4,3},{5,4},{6,5},{7,6},{0,7},{9,8},{10,9},{11,1... | collective-permute-start | bytes 589832 | tf_op jit(solution)/shard_map/ppermute | solution.py:24
  55.4 10.7 %collective-permute-done.4 = bf16[4,96,1,256]{3,1,2,0:T(8,128)(2,1)S(1)} collective-permute-done((bf16[4,96,1,256]{3,1,2,0:T(8,128)(2,1)S(1)}, bf16[4,96,1,256]{3,1,2,0:T(8,128)(2,1)S(1)}, u32[]{:S(2)}, u32[]{:S(2)}) %collective-permute-start.4) | collective-permute-done | bytes 196640 | tf_op jit(solution)/shard_map/ppermute | solution.py:22
  66.1 2.7 %collective-permute-done.5 = bf16[4,96,1,256]{3,1,2,0:T(8,128)(2,1)S(1)} collective-permute-done((bf16[4,96,1,256]{3,1,2,0:T(8,128)(2,1)S(1)}, bf16[4,96,1,256]{3,1,2,0:T(8,128)(2,1)S(1)}, u32[]{:S(2)}, u32[]{:S(2)}) %collective-permute-start.5) | collective-permute-done | bytes 196640 | tf_op jit(solution)/shard_map/ppermute | solution.py:24
  69.1 12.3 %while.41 = (s32[]{:T(128)}, f32[4,2,8,256]{3,2,1,0:T(8,128)S(1)}, bf16[4,96,10,256]{3,1,2,0:T(8,128)(2,1)S(1)}, bf16[9,2,96]{2,1,0:T(2,128)(2,1)S(1)}, s32[]{:T(128)}) while((s32[]{:T(128)}, f32[4,2,8,256]{3,2,1,0:T(8,128)S(1)}, bf16[4,96,10,256]{3,1,2,0:T(8,128)(2,1)S(1)}, bf16[9,2,96]{2,1,0:T(2,128)(2,1)S(1)}, s32[]{:T(128)}) %tuple.136), condition=%wide.region_3.4_spmd, body=%wide.region_2.3_spmd.sunk | while | flops 11829250 | bytes 11031109 | solution.py:66
  69.2 0.5 fusion.424
  72.3 0.5 fusion.424
  75.4 0.5 fusion.424
  78.4 0.5 fusion.424
  81.5 0.4 fusion.222
  81.9 0.4 convolution_bitcast_fusion.1
  82.3 0.7 multiply_convert_fusion.2
  83.0 4.9 %collective-permute-start.6 = (bf16[4,2,8,256]{3,2,1,0:T(8,128)(2,1)S(1)}, bf16[4,2,8,256]{3,2,1,0:T(8,128)(2,1)S(1)}, u32[]{:S(2)}, u32[]{:S(2)}) collective-permute-start(bf16[4,2,8,256]{3,2,1,0:T(8,128)(2,1)S(1)} %get-tuple-element.181), channel_id=1, source_target_pairs={{0,8},{8,16},{16,24},{24,32},{32,40},{40,48},{48,56},{56,64},{64,7... | collective-permute-start | bytes 98312 | tf_op jit(solution)/shard_map/ppermute | solution.py:22
  87.9 1.9 %collective-permute-start.7 = (bf16[4,2,8,256]{3,2,1,0:T(8,128)(2,1)S(1)}, bf16[4,2,8,256]{3,2,1,0:T(8,128)(2,1)S(1)}, u32[]{:S(2)}, u32[]{:S(2)}) collective-permute-start(bf16[4,2,8,256]{3,2,1,0:T(8,128)(2,1)S(1)} %get-tuple-element.181), channel_id=1, source_target_pairs={{8,0},{16,8},{24,16},{32,24},{40,32},{48,40},{56,48},{64,56},{72,6... | collective-permute-start | bytes 98312 | tf_op jit(solution)/shard_map/ppermute | solution.py:24
  89.8 6.0 %collective-permute-done.7 = bf16[4,2,8,256]{3,2,1,0:T(8,128)(2,1)S(1)} collective-permute-done((bf16[4,2,8,256]{3,2,1,0:T(8,128)(2,1)S(1)}, bf16[4,2,8,256]{3,2,1,0:T(8,128)(2,1)S(1)}, u32[]{:S(2)}, u32[]{:S(2)}) %collective-permute-start.7) | collective-permute-done | bytes 32800 | tf_op jit(solution)/shard_map/ppermute | solution.py:24
  95.9 0.8 collective-permute-start.8
  96.7 5.5 %collective-permute-start.9 = (bf16[12,2,1,256]{3,2,1,0:T(2,128)(2,1)S(1)}, bf16[12,2,1,256]{3,2,1,0:T(2,128)(2,1)S(1)}, u32[]{:S(2)}, u32[]{:S(2)}) collective-permute-start(bf16[12,2,1,256]{3,2,1,0:T(2,128)(2,1)S(1)} %get-tuple-element.236), channel_id=1, source_target_pairs={{1,0},{2,1},{3,2},{4,3},{5,4},{6,5},{7,6},{0,7},{9,8},{10,9},{11,1... | collective-permute-start | bytes 36872 | tf_op jit(solution)/shard_map/ppermute | solution.py:24
  102.2 1.2 collective-permute-done.8
  104.0 23.7 %while.42 = (s32[]{:T(128)}, bf16[4,96,8,256]{3,1,2,0:T(8,128)(2,1)S(1)}, s32[4]{0:T(128)S(1)}, bf16[12,2,10,256]{3,1,0,2:T(2,128)(2,1)S(1)}, bf16[9,96,18]{1,2,...) while((s32[]{:T(128)}, bf16[4,96,8,256]{3,1,2,0:T(8,128)(2,1)S(1)}, ...), condition=%wide.region_6.7_spmd, body=%wide.region_5.6_spmd.sunk | while | flops 67338336 | bytes 15539603 | solution.py:60
  104.0 0.6 dynamic_slice.34
  108.8 0.3 fusion.461
  109.4 0.4 fusion.462
  109.9 0.6 dynamic_slice.34
  113.7 0.3 fusion.460
  115.3 0.4 fusion.462
  115.8 0.6 dynamic_slice.34
  121.3 0.4 fusion.462
  121.7 0.6 dynamic_slice.34
  127.2 0.4 fusion.462
  127.7 2.9 %collective-permute-start.10 = (bf16[4,96,1,256]{3,1,2,0:T(8,128)(2,1)S(1)}, bf16[4,96,1,256]{3,1,2,0:T(8,128)(2,1)S(1)}, u32[]{:S(2)}, u32[]{:S(2)}) collective-permute-start(bf16[4,96,1,256]{3,1,2,0:T(8,128)(2,1)S(1)} %get-tuple-element.231), channel_id=1, source_target_pairs={{0,1},{1,2},{2,3},{3,4},{4,5},{5,6},{6,7},{7,0},{8,9},{9,10},{10,1... | collective-permute-start | bytes 589832 | tf_op jit(solution)/shard_map/ppermute | solution.py:22
  130.6 3.4 %collective-permute-start.11 = (bf16[4,96,1,256]{3,1,2,0:T(8,128)(2,1)S(1)}, bf16[4,96,1,256]{3,1,2,0:T(8,128)(2,1)S(1)}, u32[]{:S(2)}, u32[]{:S(2)}) collective-permute-start(bf16[4,96,1,256]{3,1,2,0:T(8,128)(2,1)S(1)} %get-tuple-element.232), channel_id=1, source_target_pairs={{1,0},{2,1},{3,2},{4,3},{5,4},{6,5},{7,6},{0,7},{9,8},{10,9},{11,1... | collective-permute-start | bytes 589832 | tf_op jit(solution)/shard_map/ppermute | solution.py:24
  134.0 13.3 %collective-permute-done.10 = bf16[4,96,1,256]{3,1,2,0:T(8,128)(2,1)S(1)} collective-permute-done((bf16[4,96,1,256]{3,1,2,0:T(8,128)(2,1)S(1)}, bf16[4,96,1,256]{3,1,2,0:T(8,128)(2,1)S(1)}, u32[]{:S(2)}, u32[]{:S(2)}) %collective-permute-start.10) | collective-permute-done | bytes 196640 | tf_op jit(solution)/shard_map/ppermute | solution.py:22
  147.4 4.2 %collective-permute-done.11 = bf16[4,96,1,256]{3,1,2,0:T(8,128)(2,1)S(1)} collective-permute-done((bf16[4,96,1,256]{3,1,2,0:T(8,128)(2,1)S(1)}, bf16[4,96,1,256]{3,1,2,0:T(8,128)(2,1)S(1)}, u32[]{:S(2)}, u32[]{:S(2)}) %collective-permute-start.11) | collective-permute-done | bytes 196640 | tf_op jit(solution)/shard_map/ppermute | solution.py:24
  151.9 12.3 %while.43 = (s32[]{:T(128)}, f32[4,2,8,256]{3,2,1,0:T(8,128)S(1)}, bf16[4,96,10,256]{3,1,2,0:T(8,128)(2,1)S(1)}, bf16[9,2,96]{2,1,0:T(2,128)(2,1)S(1)}, s32[]{:T(128)}) while((s32[]{:T(128)}, f32[4,2,8,256]{3,2,1,0:T(8,128)S(1)}, bf16[4,96,10,256]{3,1,2,0:T(8,128)(2,1)S(1)}, bf16[9,2,96]{2,1,0:T(2,128)(2,1)S(1)}, s32[]{:T(128)}) %tuple.137), condition=%wide.region_8.9_spmd, body=%wide.region_7.8_spmd.sunk | while | flops 11829250 | bytes 11031109 | solution.py:66
  151.9 0.5 fusion.482
  155.0 0.5 fusion.482
  158.1 0.5 fusion.482
  161.2 0.5 fusion.482
  164.2 0.4 fusion.223
  164.7 0.4 convolution_bitcast_fusion
  165.0 0.7 multiply_add_fusion
  (240 shorter events, 42.0 us)
Async XLA Ops:
  0.0 25.3 %copy-start = (bf16[9,96,18]{1,2,0:T(8,128)(2,1)S(1)}, bf16[9,96,18]{1,2,0:T(8,128)(2,1)}, u32[]{:S(2)}) copy-start(bf16[9,96,18]{1,2,0:T(8,128)(2,1)} %param.22) | copy-start | bytes 93316
  0.0 25.3 %copy-start.12 = (f32[96]{0:T(128)S(1)}, f32[96]{0:T(128)}, u32[]{:S(2)}) copy-start(f32[96]{0:T(128)} %param.24) | copy-start | bytes 1156
  0.9 4.5 %collective-permute-start = (bf16[4,2,8,256]{3,2,1,0:T(8,128)(2,1)S(1)}, bf16[4,2,8,256]{3,2,1,0:T(8,128)(2,1)S(1)}, u32[]{:S(2)}, u32[]{:S(2)}) collective-permute-start(bf16[4,2,8,256]{3,2,1,0:T(8,128)(2,1)S(1)} %multiply_convert_fusion.3), channel_id=1, source_target_pairs={{0,8},{8,16},{16,24},{24,32},{32,40},{40,48},{48,56},{56,64},{64,7... | collective-permute-start | bytes 98312 | tf_op jit(solution)/shard_map/ppermute | solution.py:22
  3.3 7.9 %collective-permute-start.1 = (bf16[4,2,8,256]{3,2,1,0:T(8,128)(2,1)S(1)}, bf16[4,2,8,256]{3,2,1,0:T(8,128)(2,1)S(1)}, u32[]{:S(2)}, u32[]{:S(2)}) collective-permute-start(bf16[4,2,8,256]{3,2,1,0:T(8,128)(2,1)S(1)} %multiply_convert_fusion.3), channel_id=1, source_target_pairs={{8,0},{16,8},{24,16},{32,24},{40,32},{48,40},{56,48},{64,56},{72,6... | collective-permute-start | bytes 98312 | tf_op jit(solution)/shard_map/ppermute | solution.py:24
  11.2 8.4 %collective-permute-start.2 = (bf16[12,2,1,256]{3,2,1,0:T(2,128)(2,1)S(1)}, bf16[12,2,1,256]{3,2,1,0:T(2,128)(2,1)S(1)}, u32[]{:S(2)}, u32[]{:S(2)}) collective-permute-start(bf16[12,2,1,256]{3,2,1,0:T(2,128)(2,1)S(1)} %get-tuple-element.237), channel_id=1, source_target_pairs={{0,1},{1,2},{2,3},{3,4},{4,5},{5,6},{6,7},{7,0},{8,9},{9,10},{10,1... | collective-permute-start | bytes 36872 | tf_op jit(solution)/shard_map/ppermute | solution.py:22
  18.3 6.6 %collective-permute-start.3 = (bf16[12,2,1,256]{3,2,1,0:T(2,128)(2,1)S(1)}, bf16[12,2,1,256]{3,2,1,0:T(2,128)(2,1)S(1)}, u32[]{:S(2)}, u32[]{:S(2)}) collective-permute-start(bf16[12,2,1,256]{3,2,1,0:T(2,128)(2,1)S(1)} %get-tuple-element.238), channel_id=1, source_target_pairs={{1,0},{2,1},{3,2},{4,3},{5,4},{6,5},{7,6},{0,7},{9,8},{10,9},{11,1... | collective-permute-start | bytes 36872 | tf_op jit(solution)/shard_map/ppermute | solution.py:24
  25.3 30.1 %copy-start.8 = (s32[1,1,256]{2,1,0:T(1,128)S(1)}, s32[1,1,256]{2,1,0:T(1,128)}, u32[]{:S(2)}) copy-start(s32[1,1,256]{2,1,0:T(1,128)} %param.27) | copy-start | bytes 3076
  25.3 30.0 %copy-start.9 = (s32[1,1,256]{2,1,0:T(1,128)S(1)}, s32[1,1,256]{2,1,0:T(1,128)}, u32[]{:S(2)}) copy-start(s32[1,1,256]{2,1,0:T(1,128)} %param.26) | copy-start | bytes 3076
  49.0 17.1 %collective-permute-start.4 = (bf16[4,96,1,256]{3,1,2,0:T(8,128)(2,1)S(1)}, bf16[4,96,1,256]{3,1,2,0:T(8,128)(2,1)S(1)}, u32[]{:S(2)}, u32[]{:S(2)}) collective-permute-start(bf16[4,96,1,256]{3,1,2,0:T(8,128)(2,1)S(1)} %get-tuple-element.233), channel_id=1, source_target_pairs={{0,1},{1,2},{2,3},{3,4},{4,5},{5,6},{6,7},{7,0},{8,9},{9,10},{10,1... | collective-permute-start | bytes 589832 | tf_op jit(solution)/shard_map/ppermute | solution.py:22
  50.3 18.5 %collective-permute-start.5 = (bf16[4,96,1,256]{3,1,2,0:T(8,128)(2,1)S(1)}, bf16[4,96,1,256]{3,1,2,0:T(8,128)(2,1)S(1)}, u32[]{:S(2)}, u32[]{:S(2)}) collective-permute-start(bf16[4,96,1,256]{3,1,2,0:T(8,128)(2,1)S(1)} %get-tuple-element.234), channel_id=1, source_target_pairs={{1,0},{2,1},{3,2},{4,3},{5,4},{6,5},{7,6},{0,7},{9,8},{10,9},{11,1... | collective-permute-start | bytes 589832 | tf_op jit(solution)/shard_map/ppermute | solution.py:24
  55.4 13.7 %copy-start.6 = (bf16[9,2,96]{2,1,0:T(2,128)(2,1)S(1)}, bf16[9,2,96]{2,1,0:T(2,128)(2,1)}, u32[]{:S(2)}) copy-start(bf16[9,2,96]{2,1,0:T(2,128)(2,1)} %param.23) | copy-start | bytes 10372
  69.1 12.4 %copy-start.2 = (f32[4,2,8,256]{3,2,1,0:T(8,128)S(1)}, f32[4,2,8,256]{3,2,1,0:T(8,128)}, u32[]{:S(2)}) copy-start(f32[4,2,8,256]{3,2,1,0:T(8,128)} %param.19) | copy-start | bytes 196612
  69.1 12.4 %copy-start.10 = (s32[1,1,256]{2,1,0:T(1,128)S(1)}, s32[1,1,256]{2,1,0:T(1,128)}, u32[]{:S(2)}) copy-start(s32[1,1,256]{2,1,0:T(1,128)} %param.28) | copy-start | bytes 3076
  69.1 12.8 %copy-start.7 = (f32[1,1,256]{2,1,0:T(1,128)S(1)}, f32[1,1,256]{2,1,0:T(1,128)}, u32[]{:S(2)}) copy-start(f32[1,1,256]{2,1,0:T(1,128)} %param.29) | copy-start | bytes 3076
  69.1 13.2 %copy-start.4 = (f32[4,2,8,256]{3,2,1,0:T(8,128)S(1)}, f32[4,2,8,256]{3,2,1,0:T(8,128)}, u32[]{:S(2)}) copy-start(f32[4,2,8,256]{3,2,1,0:T(8,128)} %param.20) | copy-start | bytes 196612
  81.5 22.4 %copy-start.1 = (bf16[9,96,18]{1,2,0:T(8,128)(2,1)S(1)}, bf16[9,96,18]{1,2,0:T(8,128)(2,1)}, u32[]{:S(2)}) copy-start(bf16[9,96,18]{1,2,0:T(8,128)(2,1)} %param.22) | copy-start | bytes 93316
  81.5 22.4 %copy-start.13 = (f32[96]{0:T(128)S(1)}, f32[96]{0:T(128)}, u32[]{:S(2)}) copy-start(f32[96]{0:T(128)} %param.24) | copy-start | bytes 1156
  83.0 6.8 %collective-permute-start.6 = (bf16[4,2,8,256]{3,2,1,0:T(8,128)(2,1)S(1)}, bf16[4,2,8,256]{3,2,1,0:T(8,128)(2,1)S(1)}, u32[]{:S(2)}, u32[]{:S(2)}) collective-permute-start(bf16[4,2,8,256]{3,2,1,0:T(8,128)(2,1)S(1)} %get-tuple-element.181), channel_id=1, source_target_pairs={{0,8},{8,16},{16,24},{24,32},{32,40},{40,48},{48,56},{56,64},{64,7... | collective-permute-start | bytes 98312 | tf_op jit(solution)/shard_map/ppermute | solution.py:22
  87.9 7.9 %collective-permute-start.7 = (bf16[4,2,8,256]{3,2,1,0:T(8,128)(2,1)S(1)}, bf16[4,2,8,256]{3,2,1,0:T(8,128)(2,1)S(1)}, u32[]{:S(2)}, u32[]{:S(2)}) collective-permute-start(bf16[4,2,8,256]{3,2,1,0:T(8,128)(2,1)S(1)} %get-tuple-element.181), channel_id=1, source_target_pairs={{8,0},{16,8},{24,16},{32,24},{40,32},{48,40},{56,48},{64,56},{72,6... | collective-permute-start | bytes 98312 | tf_op jit(solution)/shard_map/ppermute | solution.py:24
  95.9 7.6 %collective-permute-start.8 = (bf16[12,2,1,256]{3,2,1,0:T(2,128)(2,1)S(1)}, bf16[12,2,1,256]{3,2,1,0:T(2,128)(2,1)S(1)}, u32[]{:S(2)}, u32[]{:S(2)}) collective-permute-start(bf16[12,2,1,256]{3,2,1,0:T(2,128)(2,1)S(1)} %get-tuple-element.235), channel_id=1, source_target_pairs={{0,1},{1,2},{2,3},{3,4},{4,5},{5,6},{6,7},{7,0},{8,9},{9,10},{10,1... | collective-permute-start | bytes 36872 | tf_op jit(solution)/shard_map/ppermute | solution.py:22
  96.7 6.8 %collective-permute-start.9 = (bf16[12,2,1,256]{3,2,1,0:T(2,128)(2,1)S(1)}, bf16[12,2,1,256]{3,2,1,0:T(2,128)(2,1)S(1)}, u32[]{:S(2)}, u32[]{:S(2)}) collective-permute-start(bf16[12,2,1,256]{3,2,1,0:T(2,128)(2,1)S(1)} %get-tuple-element.236), channel_id=1, source_target_pairs={{1,0},{2,1},{3,2},{4,3},{5,4},{6,5},{7,6},{0,7},{9,8},{10,9},{11,1... | collective-permute-start | bytes 36872 | tf_op jit(solution)/shard_map/ppermute | solution.py:24
  127.7 19.7 %collective-permute-start.10 = (bf16[4,96,1,256]{3,1,2,0:T(8,128)(2,1)S(1)}, bf16[4,96,1,256]{3,1,2,0:T(8,128)(2,1)S(1)}, u32[]{:S(2)}, u32[]{:S(2)}) collective-permute-start(bf16[4,96,1,256]{3,1,2,0:T(8,128)(2,1)S(1)} %get-tuple-element.231), channel_id=1, source_target_pairs={{0,1},{1,2},{2,3},{3,4},{4,5},{5,6},{6,7},{7,0},{8,9},{9,10},{10,1... | collective-permute-start | bytes 589832 | tf_op jit(solution)/shard_map/ppermute | solution.py:22
  130.6 20.9 %collective-permute-start.11 = (bf16[4,96,1,256]{3,1,2,0:T(8,128)(2,1)S(1)}, bf16[4,96,1,256]{3,1,2,0:T(8,128)(2,1)S(1)}, u32[]{:S(2)}, u32[]{:S(2)}) collective-permute-start(bf16[4,96,1,256]{3,1,2,0:T(8,128)(2,1)S(1)} %get-tuple-element.232), channel_id=1, source_target_pairs={{1,0},{2,1},{3,2},{4,3},{5,4},{6,5},{7,6},{0,7},{9,8},{10,9},{11,1... | collective-permute-start | bytes 589832 | tf_op jit(solution)/shard_map/ppermute | solution.py:24
  151.8 12.4 %copy-start.3 = (f32[4,2,8,256]{3,2,1,0:T(8,128)S(1)}, f32[4,2,8,256]{3,2,1,0:T(8,128)}, u32[]{:S(2)}) copy-start(f32[4,2,8,256]{3,2,1,0:T(8,128)} %get-tuple-element.182) | copy-start | bytes 196612
  151.8 12.4 %copy-start.11 = (s32[1,1,256]{2,1,0:T(1,128)S(1)}, s32[1,1,256]{2,1,0:T(1,128)}, u32[]{:S(2)}) copy-start(s32[1,1,256]{2,1,0:T(1,128)} %param.28) | copy-start | bytes 3076
  151.9 13.2 %copy-start.5 = (f32[4,2,8,256]{3,2,1,0:T(8,128)S(1)}, f32[4,2,8,256]{3,2,1,0:T(8,128)}, u32[]{:S(2)}) copy-start(f32[4,2,8,256]{3,2,1,0:T(8,128)} %param.21) | copy-start | bytes 196612
where the time goes:
time: 166 us
  waiting for transfers between devices  49.9 us (30%)
  matrix products  43 us (26%)
  starting transfers between devices  37.5 us (23%)
  loops' own time  16.1 us (10%)
  local copies, waits for them, and re-layouts  15.1 us (9%)
  other arithmetic  3 us (2%)
    dot_general x144, matrix products, conv_three(): jnp.einsum('oc,crw->orw', weights[3 * row_off + col_off], shifted, prefer...  41.4 us
    ppermute x6, waiting for transfers between devices, with_halo(): lax.ppermute(tail, axis, [(i, (i + 1) % count) for i in range(ends)])  25.8 us
    ppermute x6, waiting for transfers between devices, with_halo(): lax.ppermute(head, axis, [((i + 1) % count, i) for i in range(ends)])  24.1 us
    ppermute x6, starting transfers between devices, with_halo(): lax.ppermute(tail, axis, [(i, (i + 1) % count) for i in range(ends)])  19.5 us
    ppermute x6, starting transfers between devices, with_halo(): lax.ppermute(head, axis, [((i + 1) % count, i) for i in range(ends)])  18.1 us
    another operation x2, loops' own time, denoise_net(): hidden = lax.map(hidden_at, jnp.arange(frames_here, dtype=jnp.int32))  15.7 us
    slice x32, local copies, waits for them, and re-layouts, conv_three(): jnp.roll(window[:, row_off:row_off + out_rows, :], 1 - col_off, axis=2)  8.35 us
    dynamic_slice x8, local copies, waits for them, and re-layouts, denoise_net(): hidden = lax.map(hidden_at, jnp.arange(frames_here, dtype=jnp.int32))  4.77 us
  transfers between devices with their start and end apart: 12, of which 10 were waited for; matrix products, arithmetic and copies ran while one was open for 0% of the time, Pallas kernels for 0%

commit v1 on v0

v1 whole, which is shorter than its diff:
```python
import functools

import jax
import jax.numpy as jnp
from jax import lax
from jax.experimental import pallas as pl
from jax.experimental.pallas import tpu as pltpu
from jax.sharding import PartitionSpec as P

MESH = pl.DeviceIdType.MESH
LEVELS = (1.0, 0.5, 0.2)
OBS_NOISE = 0.1
COVARIANCE_GAIN = 0.5
T = 4
LAYERS = 2
TL = 8
ROWS = 8
COLS = 256
HID = 96
C_IN = 18
SLOTS = 256
PAIRS = 6
BANDS = 10
K_IN = 224
SENDS = ((-1, -1), (0, -1), (1, -1), (-1, 1), (0, 1), (1, 1), (-1, 0), (1, 0))


def three_parts(values):
    high = values.astype(jnp.bfloat16).astype(jnp.float32)
    rest = values - high
    mid = rest.astype(jnp.bfloat16).astype(jnp.float32)
    return high, mid, rest - mid


def build_conv_in(w1_raw, embed_raw, w1):
    lane = lax.broadcasted_iota(jnp.int32, (HID, 256), 1)
    base = jnp.zeros((HID, 256), jnp.float32)
    for off in range(9):
        slab = jnp.concatenate(
            [w1_raw[off].astype(jnp.float32) * 0.5, jnp.zeros((HID, 256 - C_IN), jnp.float32)], axis=1
        )
        base = base + (pltpu.roll(slab, 24 * off, 1) if off else slab)
    diagonal = lax.broadcasted_iota(jnp.int32, (HID, HID), 0) == lax.broadcasted_iota(
        jnp.int32, (HID, HID), 1
    )
    embed = jnp.sum(
        jnp.where(diagonal, jnp.broadcast_to(embed_raw[...], (HID, HID)), 0.0), axis=1, keepdims=True
    )
    parts = three_parts(embed * 0.5)
    for t in range(T):
        shifted = pltpu.roll(base, 2 * t, 1) if t else base
        for piece in range(3):
            shifted = jnp.where(lane == 216 + piece, parts[piece], shifted)
        w1[t * HID : (t + 1) * HID, :] = shifted[:, :K_IN].astype(jnp.bfloat16)


def build_conv_out(w2_raw, w2):
    sub = lax.broadcasted_iota(jnp.int32, (TL, HID), 0)
    pieces = []
    for b in range(3):
        for a in range(3):
            taps = w2_raw[3 * a + b].astype(jnp.float32)
            pieces.append(
                jnp.where(
                    sub % 2 == 0,
                    jnp.broadcast_to(taps[0:1], (TL, HID)),
                    jnp.broadcast_to(taps[1:2], (TL, HID)),
                )
            )
    tall = jnp.concatenate(pieces, axis=0)
    wide = jnp.concatenate([tall, jnp.zeros((72, T * HID - HID), jnp.float32)], axis=1)
    state = (lax.broadcasted_iota(jnp.int32, (72, T * HID), 0) % TL) // 2
    total = jnp.where(state == 0, wide, 0.0)
    for t in range(1, T):
        total = total + jnp.where(state == t, pltpu.roll(wide, t * HID, 1), 0.0)
    w2[...] = total.astype(jnp.bfloat16)


def build_guide(count, obs_step, obs_row, obs_col, obs_value, guide):
    slot = lax.broadcasted_iota(jnp.int32, (1, SLOTS), 1)
    live = slot < count[...]
    cell = jnp.where(live, obs_row[...] * TL + obs_step[...] * LAYERS, -1)
    hot = lax.broadcasted_iota(jnp.int32, (ROWS * TL, SLOTS), 0) == cell
    high, mid, low = three_parts(obs_value[...])
    left = jnp.concatenate(
        [
            jnp.where(hot, 1.0, 0.0),
            jnp.where(hot, high, 0.0),
            jnp.where(hot, mid, 0.0),
            jnp.where(hot, low, 0.0),
        ],
        axis=0,
    ).astype(jnp.bfloat16)
    right = jnp.where(
        lax.broadcasted_iota(jnp.int32, (COLS, SLOTS), 0) == obs_col[...], 1.0, 0.0
    ).astype(jnp.bfloat16)
    found = lax.dot_general(left, right, (((1,), (1,)), ((), ())), preferred_element_type=jnp.float32)
    rows = ROWS * TL
    guide[0:rows, :] = found[0:rows]
    guide[rows : 2 * rows, :] = (
        found[rows : 2 * rows] + found[2 * rows : 3 * rows] + found[3 * rows : 4 * rows]
    )


def kernel(
    sizes,
    x_hbm,
    first_hbm,
    second_hbm,
    w1_hbm,
    w2_hbm,
    embed_hbm,
    count_hbm,
    step_hbm,
    row_hbm,
    col_hbm,
    value_hbm,
    out,
    x_in,
    first,
    second,
    w1_raw,
    w2_raw,
    embed_raw,
    count,
    obs_step,
    obs_row,
    obs_col,
    obs_value,
    state,
    w1,
    w2,
    guide,
    tiles,
    frames,
    taps,
    load_sems,
    send_sems,
    recv_sems,
):
    n_tm, n_rows = sizes
    tm = lax.axis_index("tm")
    rw = lax.axis_index("rows")

    def peer(dt, dr):
        return {
            "tm": lax.rem(tm + dt + n_tm, n_tm) if dt else tm,
            "rows": lax.rem(rw + dr + n_rows, n_rows) if dr else rw,
        }

    barrier = pltpu.get_barrier_semaphore()
    for dt, dr in SENDS:
        pl.semaphore_signal(barrier, inc=1, device_id=peer(dt, dr), device_id_type=MESH)

    loads = [
        pltpu.make_async_copy(src, dst, load_sems.at[i])
        for i, (src, dst) in enumerate(
            (
                (x_hbm, x_in),
                (w1_hbm, w1_raw),
                (embed_hbm, embed_raw),
                (w2_hbm, w2_raw),
                (count_hbm, count),
                (step_hbm, obs_step),
                (row_hbm, obs_row),
                (col_hbm, obs_col),
                (value_hbm, obs_value),
                (first_hbm, first),
                (second_hbm, second),
            )
        )
    ]
    for load in loads:
        load.start()

    def send(index):
        copies = []
        for k, (dt, dr) in enumerate(SENDS):
            source = {0: slice(1, 5), 1: slice(4, 5), -1: slice(1, 2)}[dr]
            target = {0: slice(1, 5), 1: slice(0, 1), -1: slice(5, 6)}[dr]
            copies.append(
                pltpu.make_async_remote_copy(
                    src_ref=tiles.at[index, 1, source],
                    dst_ref=tiles.at[index, 1 - dt, target],
                    send_sem=send_sems.at[index, k],
                    recv_sem=recv_sems.at[index, k],
                    device_id=peer(dt, dr),
                    device_id_type=MESH,
                )
            )
        for copy in copies:
            copy.start()
        return copies

    def put_tiles(index, pair, upper, lower):
        scale = 1.0 / (1.0 + LEVELS[index] ** 2) ** 0.5
        tile = jnp.concatenate([upper, lower], axis=0) * scale
        tiles[index, 1, pair + 1] = tile.astype(jnp.bfloat16)

    def unpack(index, pair, block):
        tile = tiles[index, block, pair].astype(jnp.float32)
        if block == 0:
            tile = jnp.where(tm == 0, 0.0, tile)
        if block == 2:
            tile = jnp.where(tm == n_tm - 1, 0.0, tile)
        for b in range(3):
            moved = pltpu.roll(tile, (1 - b) % COLS, 1) if b != 1 else tile
            for half in range(2):
                at = (2 * pair + half) * 72 + b * 24 + block * 8
                frames[at : at + 8, :] = moved[half * 8 : half * 8 + 8]

    def hidden_band(index, j):
        window = frames[pl.ds(pl.multiple_of(72 * j, 8), 216), :]
        ones = jnp.full((K_IN - 216, COLS), LEVELS[index], jnp.float32)
        window = jnp.concatenate([window, ones], axis=0).astype(jnp.bfloat16)
        half = jnp.dot(w1[...], window, preferred_element_type=jnp.float32)
        hidden = (half + half * jnp.tanh(half)).astype(jnp.bfloat16)
        taps[j] = jnp.dot(w2[...], hidden, preferred_element_type=jnp.float32)

    def finish_row(index, r, noise):
        level_now, level_next = LEVELS[index], LEVELS[index + 1]
        sums = []
        for b in range(3):
            at = b * 24
            sums.append(
                taps[r, at : at + 8, :] + taps[r + 1, at + 8 : at + 16, :] + taps[r + 2, at + 16 : at + 24, :]
            )
        net = sums[1] + pltpu.roll(sums[0], 1, 1) + pltpu.roll(sums[2], COLS - 1, 1)
        current = state[r]
        base = 1.0 + level_now**2
        denoised = current * (1.0 / base) + (level_now / base**0.5) * net
        hits = guide[r * 8 : r * 8 + 8, :]
        values = guide[64 + r * 8 : 64 + r * 8 + 8, :]
        misfit = (values - hits * denoised) * (1.0 / (OBS_NOISE + COVARIANCE_GAIN * level_now**2))
        score = (denoised - current) * (1.0 / level_now**2) + misfit
        spread = level_now**2 - level_next**2
        return current + spread * score + spread**0.5 * noise[r]

    loads[0].wait()
    state[...] = jnp.swapaxes(x_in[...].reshape(TL, ROWS, COLS), 0, 1)
    for pair in range(4):
        put_tiles(0, pair, state[2 * pair], state[2 * pair + 1])
    pl.semaphore_wait(barrier, len(SENDS))
    copies = send(0)

    for load in loads[1:4]:
        load.wait()
    build_conv_in(w1_raw, embed_raw, w1)
    build_conv_out(w2_raw, w2)
    for load in loads[4:]:
        load.wait()
    build_guide(count, obs_step, obs_row, obs_col, obs_value, guide)
    turned_first = jnp.swapaxes(first[...].reshape(TL, ROWS, COLS), 0, 1)
    turned_second = jnp.swapaxes(second[...].reshape(TL, ROWS, COLS), 0, 1)

    for index in range(2):
        for pair in range(1, 5):
            unpack(index, pair, 1)
        for copy in copies:
            copy.wait_recv()
        for pair in range(1, 5):
            unpack(index, pair, 0)
            unpack(index, pair, 2)
        for block in range(3):
            unpack(index, 0, block)
            unpack(index, 5, block)

        def band(j, carry):
            hidden_band(index, j)
            return carry

        lax.fori_loop(0, BANDS, band, 0)
        for copy in copies:
            copy.wait_send()
        if index == 0:
            for pair in range(4):
                slabs = [finish_row(index, 2 * pair + half, turned_first) for half in range(2)]
                for half in range(2):
                    state[2 * pair + half] = slabs[half]
                put_tiles(1, pair, *slabs)
            copies = send(1)
        else:
            done = jnp.stack([finish_row(index, r, turned_second) for r in range(ROWS)], axis=0)
            out[...] = jnp.swapaxes(done, 0, 1).reshape(TL * ROWS, COLS)


def per_device(
    sizes,
    noisy_states,
    noise_first,
    noise_second,
    conv_in,
    conv_out,
    level_embed,
    obs_count,
    obs_step,
    obs_row,
    obs_col,
    obs_value,
):
    flat = (TL * ROWS, COLS)
    slots = (1, SLOTS)
    any_space = pl.BlockSpec(memory_space=pl.ANY)
    result = pl.pallas_call(
        functools.partial(kernel, sizes),
        out_shape=jax.ShapeDtypeStruct(flat, jnp.float32),
        in_specs=[any_space] * 11,
        out_specs=pl.BlockSpec(memory_space=pltpu.VMEM),
        scratch_shapes=[
            pltpu.VMEM(flat, jnp.float32),
            pltpu.VMEM(flat, jnp.float32),
            pltpu.VMEM(flat, jnp.float32),
            pltpu.VMEM((9, HID, C_IN), jnp.bfloat16),
            pltpu.VMEM((9, LAYERS, HID), jnp.bfloat16),
            pltpu.VMEM((1, HID), jnp.float32),
            pltpu.VMEM((1, 1), jnp.int32),
            pltpu.VMEM(slots, jnp.int32),
            pltpu.VMEM(slots, jnp.int32),
            pltpu.VMEM(slots, jnp.int32),
            pltpu.VMEM(slots, jnp.float32),
            pltpu.VMEM((ROWS, TL, COLS), jnp.float32),
            pltpu.VMEM((T * HID, K_IN), jnp.bfloat16),
            pltpu.VMEM((72, T * HID), jnp.bfloat16),
            pltpu.VMEM((2 * ROWS * TL, COLS), jnp.float32),
            pltpu.VMEM((2, 3, PAIRS, 16, COLS), jnp.bfloat16),
            pltpu.VMEM((2 * PAIRS * 72, COLS), jnp.float32),
            pltpu.VMEM((BANDS, 72, COLS), jnp.float32),
            pltpu.SemaphoreType.DMA((11,)),
            pltpu.SemaphoreType.DMA((2, len(SENDS))),
            pltpu.SemaphoreType.DMA((2, len(SENDS))),
        ],
        compiler_params=pltpu.CompilerParams(
            collective_id=0, has_side_effects=True, vmem_limit_bytes=32 * 1024 * 1024
        ),
        name="reverse_steps",
    )(
        noisy_states.reshape(flat),
        noise_first.reshape(flat),
        noise_second.reshape(flat),
        conv_in,
        conv_out,
        level_embed.reshape(1, HID),
        obs_count,
        obs_step.reshape(slots),
        obs_row.reshape(slots),
        obs_col.reshape(slots),
        obs_value.reshape(slots),
    )
    return result.reshape(noisy_states.shape)


def solution(mesh):
    sizes = (mesh.shape["tm"], mesh.shape["rows"])
    cells = P("tm", None, "rows", None)
    block = P("tm", "rows", None)
    return jax.shard_map(
        functools.partial(per_device, sizes),
        mesh=mesh,
        in_specs=(cells, cells, cells, P(), P(), P(), P("tm", "rows"), block, block, block, block),
        out_specs=cells,
        check_vma=False,
    )
```

time: 166 us -> 34.3 us (0.21)
  the two profiles are of different devices: /device:TPU:99 before, /device:TPU:1 now
where the time goes in v1:
time: 34.3 us; the launch traced here: 34.2 us
  Pallas kernels  31.6 us (92%)
  local copies, waits for them, and re-layouts  1.77 us (5%)
  between operations  0.8 us (2%)
    pallas_call x1, Pallas kernels, per_device(): pl.pallas_call(functools.partial(kernel, sizes), out_shape=jax.ShapeDtype...  31.6 us
    unnamed x20, local copies, waits for them, and re-layouts  1.77 us

profile of v1, /device:TPU:1, one launch (start us, length us, event | category | flops | bytes accessed | tf_op | source)
XLA Modules:
  0.0 34.2 jit_solution(9914381190477588844)
XLA Ops:
  0.7 0.0 copy-start
  0.7 0.0 copy-start.1
  0.7 0.0 copy-start.2
  0.7 0.0 copy-start.3
  0.7 0.0 copy-start.4
  0.7 0.0 copy-start.5
  0.7 0.0 copy-start.6
  0.7 0.0 copy-start.7
  0.7 0.0 copy-start.8
  0.7 1.1 %copy.12.w1_hbm = bf16[9,96,18]{2,1,0:T(8,128)(2,1)S(1)} copy(bf16[9,96,18]{1,2,0:T(8,128)(2,1)} %param.14) | data formatting | bytes 62208 | tf_op args[3]
  1.8 0.0 copy-done
  1.9 0.0 copy-done.1
  1.9 0.0 copy-done.2
  1.9 0.0 copy-done.3
  1.9 0.0 copy-done.4
  1.9 0.0 copy-done.5
  1.9 0.0 copy-done.6
  1.9 0.0 copy-done.7
  1.9 0.0 copy-done.8
  1.9 31.6 %reverse_steps.1 = f32[64,256]{1,0:T(8,128)S(1)} custom-call(f32[64,256]{1,0:T(8,128)S(1)} %bitcast.10, f32[64,256]{1,0:T(8,128)S(1)} %bitcast.11, f32[64,256]{1,0:T(8,128)S(1)} %bitcast.12, bf16[9,96,18]{2,1,0:T(8,128)(2,1)S(1)} %copy.12.w1_hbm, bf16[9,2,96]{2,1,0:T(2,128)(2,1)S(1)} %copy-done.3, f32[1,96]{1,0:T(1,128)S(1)} %bitcast.17, ...), custom_call_target="tpu_custom_call" | custom-call | tf_op jit(solution)/shard_map/reverse_steps/pallas_call | solution.py:304
  33.6 0.6 %copy.15 = f32[4,2,8,256]{3,2,1,0:T(8,128)} copy(f32[4,2,8,256]{3,2,1,0:T(8,128)S(1)} %bitcast.9) | data formatting | bytes 131072
Async XLA Ops:
  0.7 1.2 %copy-start = (f32[4,2,8,256]{3,2,1,0:T(8,128)S(1)}, f32[4,2,8,256]{3,2,1,0:T(8,128)}, u32[]{:S(2)}) copy-start(f32[4,2,8,256]{3,2,1,0:T(8,128)} %param.11) | copy-start | bytes 196612
  0.7 1.2 %copy-start.1 = (f32[4,2,8,256]{3,2,1,0:T(8,128)S(1)}, f32[4,2,8,256]{3,2,1,0:T(8,128)}, u32[]{:S(2)}) copy-start(f32[4,2,8,256]{3,2,1,0:T(8,128)} %param.12) | copy-start | bytes 196612
  0.7 1.2 %copy-start.2 = (f32[4,2,8,256]{3,2,1,0:T(8,128)S(1)}, f32[4,2,8,256]{3,2,1,0:T(8,128)}, u32[]{:S(2)}) copy-start(f32[4,2,8,256]{3,2,1,0:T(8,128)} %param.13) | copy-start | bytes 196612
  0.7 1.2 %copy-start.3 = (bf16[9,2,96]{2,1,0:T(2,128)(2,1)S(1)}, bf16[9,2,96]{2,1,0:T(2,128)(2,1)}, u32[]{:S(2)}) copy-start(bf16[9,2,96]{2,1,0:T(2,128)(2,1)} %w2_hbm.1) | copy-start | bytes 10372
  0.7 1.2 %copy-start.4 = (s32[1,1,256]{2,1,0:T(1,128)S(1)}, s32[1,1,256]{2,1,0:T(1,128)}, u32[]{:S(2)}) copy-start(s32[1,1,256]{2,1,0:T(1,128)} %param.18) | copy-start | bytes 3076
  0.7 1.2 %copy-start.5 = (s32[1,1,256]{2,1,0:T(1,128)S(1)}, s32[1,1,256]{2,1,0:T(1,128)}, u32[]{:S(2)}) copy-start(s32[1,1,256]{2,1,0:T(1,128)} %param.19) | copy-start | bytes 3076
  0.7 1.2 %copy-start.6 = (s32[1,1,256]{2,1,0:T(1,128)S(1)}, s32[1,1,256]{2,1,0:T(1,128)}, u32[]{:S(2)}) copy-start(s32[1,1,256]{2,1,0:T(1,128)} %param.20) | copy-start | bytes 3076
  0.7 1.2 %copy-start.7 = (f32[1,1,256]{2,1,0:T(1,128)S(1)}, f32[1,1,256]{2,1,0:T(1,128)}, u32[]{:S(2)}) copy-start(f32[1,1,256]{2,1,0:T(1,128)} %param.21) | copy-start | bytes 3076
  0.7 1.2 %copy-start.8 = (f32[96]{0:T(128)S(1)}, f32[96]{0:T(128)}, u32[]{:S(2)}) copy-start(f32[96]{0:T(128)} %param.16) | copy-start | bytes 1156

commit v2 on v1

--- a/solution.py
+++ b/solution.py
@@ -22,7 +22,17 @@
 PAIRS = 6
 BANDS = 10
 K_IN = 224
-SENDS = ((-1, -1), (0, -1), (1, -1), (-1, 1), (0, 1), (1, 1), (-1, 0), (1, 0))
+NEIGHBOURS = ((0, -1), (0, 1), (-1, -1), (1, -1), (-1, 1), (1, 1), (-1, 0), (1, 0))
+SLOT_OF = (0, 1, 4, 5, 2, 3)
+ROWS_SENDS = tuple(
+    (dt, dr, slice(1, 2) if dr < 0 else slice(2, 3), slice(3, 4) if dr < 0 else slice(0, 1))
+    for dt, dr in NEIGHBOURS[:6]
+)
+EDGE_SENDS = tuple((dt, 0, slice(1, 3), slice(1, 3)) for dt in (-1, 1))
+MID_SENDS = tuple((dt, 0, slice(4, 6), slice(4, 6)) for dt in (-1, 1))
+SENDS = ROWS_SENDS + EDGE_SENDS + MID_SENDS
+INNER_BANDS = (4, 5, 2, 3, 6, 7)
+OUTER_BANDS = (0, 1, 8, 9)
 
 
 def three_parts(values):
@@ -32,25 +42,17 @@
     return high, mid, rest - mid
 
 
-def build_conv_in(w1_raw, embed_raw, w1):
+def build_conv_in(w1_raw, embed_raw, w1_turned, w1):
+    w1_turned[...] = jnp.zeros(w1_turned.shape, jnp.float32)
+    for off in range(9):
+        w1_turned[24 * off : 24 * off + C_IN, 0:HID] = w1_raw[off].astype(jnp.float32) * 0.5
+    parts = three_parts(embed_raw[...] * 0.5)
+    for piece in range(3):
+        w1_turned[216 + piece : 217 + piece, 0:HID] = parts[piece]
+    base = jnp.transpose(w1_turned[...])[:HID]
     lane = lax.broadcasted_iota(jnp.int32, (HID, 256), 1)
-    base = jnp.zeros((HID, 256), jnp.float32)
-    for off in range(9):
-        slab = jnp.concatenate(
-            [w1_raw[off].astype(jnp.float32) * 0.5, jnp.zeros((HID, 256 - C_IN), jnp.float32)], axis=1
-        )
-        base = base + (pltpu.roll(slab, 24 * off, 1) if off else slab)
-    diagonal = lax.broadcasted_iota(jnp.int32, (HID, HID), 0) == lax.broadcasted_iota(
-        jnp.int32, (HID, HID), 1
-    )
-    embed = jnp.sum(
-        jnp.where(diagonal, jnp.broadcast_to(embed_raw[...], (HID, HID)), 0.0), axis=1, keepdims=True
-    )
-    parts = three_parts(embed * 0.5)
     for t in range(T):
-        shifted = pltpu.roll(base, 2 * t, 1) if t else base
-        for piece in range(3):
-            shifted = jnp.where(lane == 216 + piece, parts[piece], shifted)
+        shifted = jnp.where(lane < 216, pltpu.roll(base, 2 * t, 1), base) if t else base
         w1[t * HID : (t + 1) * HID, :] = shifted[:, :K_IN].astype(jnp.bfloat16)
 
 
@@ -78,7 +80,7 @@
 
 def build_guide(count, obs_step, obs_row, obs_col, obs_value, guide):
     slot = lax.broadcasted_iota(jnp.int32, (1, SLOTS), 1)
-    live = slot < count[...]
+    live = slot < count[0, 0]
     cell = jnp.where(live, obs_row[...] * TL + obs_step[...] * LAYERS, -1)
     hot = lax.broadcasted_iota(jnp.int32, (ROWS * TL, SLOTS), 0) == cell
     high, mid, low = three_parts(obs_value[...])
@@ -110,7 +112,7 @@
     w1_hbm,
     w2_hbm,
     embed_hbm,
-    count_hbm,
+    count,
     step_hbm,
     row_hbm,
     col_hbm,
@@ -122,12 +124,14 @@
     w1_raw,
     w2_raw,
     embed_raw,
-    count,
     obs_step,
     obs_row,
     obs_col,
     obs_value,
     state,
+    turned_first,
+    turned_second,
+    w1_turned,
     w1,
     w2,
     guide,
@@ -149,7 +153,7 @@
         }
 
     barrier = pltpu.get_barrier_semaphore()
-    for dt, dr in SENDS:
+    for dt, dr in NEIGHBOURS:
         pl.semaphore_signal(barrier, inc=1, device_id=peer(dt, dr), device_id_type=MESH)
 
     loads = [
@@ -160,7 +164,6 @@
                 (w1_hbm, w1_raw),
                 (embed_hbm, embed_raw),
                 (w2_hbm, w2_raw),
-                (count_hbm, count),
                 (step_hbm, obs_step),
                 (row_hbm, obs_row),
                 (col_hbm, obs_col),
@@ -173,32 +176,28 @@
     for load in loads:
         load.start()
 
-    def send(index):
-        copies = []
-        for k, (dt, dr) in enumerate(SENDS):
-            source = {0: slice(1, 5), 1: slice(4, 5), -1: slice(1, 2)}[dr]
-            target = {0: slice(1, 5), 1: slice(0, 1), -1: slice(5, 6)}[dr]
-            copies.append(
-                pltpu.make_async_remote_copy(
-                    src_ref=tiles.at[index, 1, source],
-                    dst_ref=tiles.at[index, 1 - dt, target],
-                    send_sem=send_sems.at[index, k],
-                    recv_sem=recv_sems.at[index, k],
-                    device_id=peer(dt, dr),
-                    device_id_type=MESH,
-                )
-            )
-        for copy in copies:
-            copy.start()
-        return copies
+    copies = [
+        [
+            pltpu.make_async_remote_copy(
+                src_ref=tiles.at[index, 1, source],
+                dst_ref=tiles.at[index, 1 - dt, target],
+                send_sem=send_sems.at[index, k],
+                recv_sem=recv_sems.at[index, k],
+                device_id=peer(dt, dr),
+                device_id_type=MESH,
+            )
+            for k, (dt, dr, source, target) in enumerate(SENDS)
+        ]
+        for index in range(2)
+    ]
 
     def put_tiles(index, pair, upper, lower):
         scale = 1.0 / (1.0 + LEVELS[index] ** 2) ** 0.5
         tile = jnp.concatenate([upper, lower], axis=0) * scale
-        tiles[index, 1, pair + 1] = tile.astype(jnp.bfloat16)
+        tiles[index, 1, SLOT_OF[pair + 1]] = tile.astype(jnp.bfloat16)
 
     def unpack(index, pair, block):
-        tile = tiles[index, block, pair].astype(jnp.float32)
+        tile = tiles[index, block, SLOT_OF[pair]].astype(jnp.float32)
         if block == 0:
             tile = jnp.where(tm == 0, 0.0, tile)
         if block == 2:
@@ -210,9 +209,8 @@
                 frames[at : at + 8, :] = moved[half * 8 : half * 8 + 8]
 
     def hidden_band(index, j):
-        window = frames[pl.ds(pl.multiple_of(72 * j, 8), 216), :]
         ones = jnp.full((K_IN - 216, COLS), LEVELS[index], jnp.float32)
-        window = jnp.concatenate([window, ones], axis=0).astype(jnp.bfloat16)
+        window = jnp.concatenate([frames[72 * j : 72 * j + 216, :], ones], axis=0).astype(jnp.bfloat16)
         half = jnp.dot(w1[...], window, preferred_element_type=jnp.float32)
         hidden = (half + half * jnp.tanh(half)).astype(jnp.bfloat16)
         taps[j] = jnp.dot(w2[...], hidden, preferred_element_type=jnp.float32)
@@ -236,52 +234,73 @@
         spread = level_now**2 - level_next**2
         return current + spread * score + spread**0.5 * noise[r]
 
+    def step_pair(pair):
+        slabs = [finish_row(0, 2 * pair + half, turned_first) for half in range(2)]
+        put_tiles(1, pair, *slabs)
+        for half in range(2):
+            state[2 * pair + half] = slabs[half]
+
+    n_rows_sends = len(ROWS_SENDS)
+
+    def exchange_inner(index):
+        for pair in range(1, 5):
+            unpack(index, pair, 1)
+        for copy in copies[index][n_rows_sends:]:
+            copy.wait_recv()
+        for pair in range(1, 5):
+            unpack(index, pair, 0)
+            unpack(index, pair, 2)
+
+    def exchange_outer(index):
+        for copy in copies[index][:n_rows_sends]:
+            copy.wait_recv()
+        for block in range(3):
+            unpack(index, 0, block)
+            unpack(index, 5, block)
+
     loads[0].wait()
     state[...] = jnp.swapaxes(x_in[...].reshape(TL, ROWS, COLS), 0, 1)
     for pair in range(4):
         put_tiles(0, pair, state[2 * pair], state[2 * pair + 1])
-    pl.semaphore_wait(barrier, len(SENDS))
-    copies = send(0)
-
     for load in loads[1:4]:
         load.wait()
-    build_conv_in(w1_raw, embed_raw, w1)
+    build_conv_in(w1_raw, embed_raw, w1_turned, w1)
     build_conv_out(w2_raw, w2)
+    pl.semaphore_wait(barrier, len(NEIGHBOURS))
+    for copy in copies[0]:
+        copy.start()
     for load in loads[4:]:
         load.wait()
     build_guide(count, obs_step, obs_row, obs_col, obs_value, guide)
-    turned_first = jnp.swapaxes(first[...].reshape(TL, ROWS, COLS), 0, 1)
-    turned_second = jnp.swapaxes(second[...].reshape(TL, ROWS, COLS), 0, 1)
-
+    turned_first[...] = jnp.swapaxes(first[...].reshape(TL, ROWS, COLS), 0, 1)
+    turned_second[...] = jnp.swapaxes(second[...].reshape(TL, ROWS, COLS), 0, 1)
+
+    exchange_inner(0)
+    for j in INNER_BANDS:
+        hidden_band(0, j)
+    for pair in (1, 2):
+        step_pair(pair)
+    for copy in copies[1][n_rows_sends + 2 :]:
+        copy.start()
+    exchange_outer(0)
+    for j in OUTER_BANDS:
+        hidden_band(0, j)
+    for pair in (0, 3):
+        step_pair(pair)
+    for copy in copies[1][: n_rows_sends + 2]:
+        copy.start()
+
+    exchange_inner(1)
+    for j in INNER_BANDS:
+        hidden_band(1, j)
+    exchange_outer(1)
+    for j in OUTER_BANDS:
+        hidden_band(1, j)
+    done = jnp.stack([finish_row(1, r, turned_second) for r in range(ROWS)], axis=0)
+    out[...] = jnp.swapaxes(done, 0, 1).reshape(TL * ROWS, COLS)
     for index in range(2):
-        for pair in range(1, 5):
-            unpack(index, pair, 1)
-        for copy in copies:
-            copy.wait_recv()
-        for pair in range(1, 5):
-            unpack(index, pair, 0)
-            unpack(index, pair, 2)
-        for block in range(3):
-            unpack(index, 0, block)
-            unpack(index, 5, block)
-
-        def band(j, carry):
-            hidden_band(index, j)
-            return carry
-
-        lax.fori_loop(0, BANDS, band, 0)
-        for copy in copies:
+        for copy in copies[index]:
             copy.wait_send()
-        if index == 0:
-            for pair in range(4):
-                slabs = [finish_row(index, 2 * pair + half, turned_first) for half in range(2)]
-                for half in range(2):
-                    state[2 * pair + half] = slabs[half]
-                put_tiles(1, pair, *slabs)
-            copies = send(1)
-        else:
-            done = jnp.stack([finish_row(index, r, turned_second) for r in range(ROWS)], axis=0)
-            out[...] = jnp.swapaxes(done, 0, 1).reshape(TL * ROWS, COLS)
 
 
 def per_device(
@@ -300,32 +319,34 @@
 ):
     flat = (TL * ROWS, COLS)
     slots = (1, SLOTS)
-    any_space = pl.BlockSpec(memory_space=pl.ANY)
+    far = pl.BlockSpec(memory_space=pltpu.HBM)
     result = pl.pallas_call(
         functools.partial(kernel, sizes),
-        out_shape=jax.ShapeDtypeStruct(flat, jnp.float32),
-        in_specs=[any_space] * 11,
+        out_shape=pltpu.VMEM(flat, jnp.float32),
+        in_specs=[far] * 6 + [pl.BlockSpec(memory_space=pltpu.SMEM)] + [far] * 4,
         out_specs=pl.BlockSpec(memory_space=pltpu.VMEM),
         scratch_shapes=[
             pltpu.VMEM(flat, jnp.float32),
             pltpu.VMEM(flat, jnp.float32),
             pltpu.VMEM(flat, jnp.float32),
-            pltpu.VMEM((9, HID, C_IN), jnp.bfloat16),
+            pltpu.VMEM((9, C_IN, HID), jnp.bfloat16),
             pltpu.VMEM((9, LAYERS, HID), jnp.bfloat16),
             pltpu.VMEM((1, HID), jnp.float32),
-            pltpu.VMEM((1, 1), jnp.int32),
             pltpu.VMEM(slots, jnp.int32),
             pltpu.VMEM(slots, jnp.int32),
             pltpu.VMEM(slots, jnp.int32),
             pltpu.VMEM(slots, jnp.float32),
             pltpu.VMEM((ROWS, TL, COLS), jnp.float32),
+            pltpu.VMEM((ROWS, TL, COLS), jnp.float32),
+            pltpu.VMEM((ROWS, TL, COLS), jnp.float32),
+            pltpu.VMEM((256, 128), jnp.float32),
             pltpu.VMEM((T * HID, K_IN), jnp.bfloat16),
             pltpu.VMEM((72, T * HID), jnp.bfloat16),
             pltpu.VMEM((2 * ROWS * TL, COLS), jnp.float32),
             pltpu.VMEM((2, 3, PAIRS, 16, COLS), jnp.bfloat16),
             pltpu.VMEM((2 * PAIRS * 72, COLS), jnp.float32),
             pltpu.VMEM((BANDS, 72, COLS), jnp.float32),
-            pltpu.SemaphoreType.DMA((11,)),
+            pltpu.SemaphoreType.DMA((10,)),
             pltpu.SemaphoreType.DMA((2, len(SENDS))),
             pltpu.SemaphoreType.DMA((2, len(SENDS))),
         ],
@@ -334,17 +355,22 @@
         ),
         name="reverse_steps",
     )(
-        noisy_states.reshape(flat),
-        noise_first.reshape(flat),
-        noise_second.reshape(flat),
-        conv_in,
-        conv_out,
-        level_embed.reshape(1, HID),
-        obs_count,
-        obs_step.reshape(slots),
-        obs_row.reshape(slots),
-        obs_col.reshape(slots),
-        obs_value.reshape(slots),
+        *(
+            operand if operand is obs_count else pltpu.with_memory_space_constraint(operand, pltpu.HBM)
+            for operand in (
+                noisy_states.reshape(flat),
+                noise_first.reshape(flat),
+                noise_second.reshape(flat),
+                jnp.swapaxes(conv_in, 1, 2),
+                conv_out,
+                level_embed.reshape(1, HID),
+                obs_count,
+                obs_step.reshape(slots),
+                obs_row.reshape(slots),
+                obs_col.reshape(slots),
+                obs_value.reshape(slots),
+            )
+        )
     )
     return result.reshape(noisy_states.shape)
 

time: 34.3 us -> 27.6 us (0.80)
  Pallas kernels: 31.6 us -> 26.2 us
  local copies, waits for them, and re-layouts: 1.77 us -> 0.63 us
    pallas_call x1, Pallas kernels: 31.6 us -> 26.2 us  [per_device(): pl.pallas_call(functools.partial(kernel, sizes), out_shape=pltpu.VMEM(fla...]
    unnamed x20 -> x1, local copies, waits for them, and re-layouts: 1.77 us -> 0.63 us
where the time goes in v2:
time: 27.6 us; the launch traced here: 27.5 us
  Pallas kernels  26.2 us (95%)
  between operations  0.66 us (2%)
  local copies, waits for them, and re-layouts  0.63 us (2%)
    pallas_call x1, Pallas kernels, per_device(): pl.pallas_call(functools.partial(kernel, sizes), out_shape=pltpu.VMEM(fla...  26.2 us
    unnamed x1, local copies, waits for them, and re-layouts  0.63 us

profile of v2, /device:TPU:1, one launch (start us, length us, event | category | flops | bytes accessed | tf_op | source)
XLA Modules:
  0.0 27.5 jit_solution(11985291886191340435)
XLA Ops:
  0.7 26.2 %reverse_steps.1 = f32[64,256]{1,0:T(8,128)S(1)} custom-call(f32[64,256]{1,0:T(8,128)} %bitcast.11, f32[64,256]{1,0:T(8,128)} %bitcast.12, f32[64,256]{1,0:T(8,128)} %bitcast.13, bf16[9,18,96]{2,1,0:T(8,128)(2,1)} %bitcast.14, bf16[9,2,96]{2,1,0:T(2,128)(2,1)} %w2_hbm.1, f32[1,96]{1,0:T(1,128)} %bitcast.19, s32[1,1]{1,0:T(1,128)S(6)} %copy.14.count, ...), custom_call_target="tpu_custom_call" | custom-call | tf_op jit(solution)/shard_map/reverse_steps/pallas_call | solution.py:323
  26.9 0.6 %copy.13 = f32[4,2,8,256]{3,2,1,0:T(8,128)} copy(f32[4,2,8,256]{3,2,1,0:T(8,128)S(1)} %bitcast.10) | data formatting | bytes 131072

commit v3 on v2

--- a/solution.py
+++ b/solution.py
@@ -19,20 +19,16 @@
 HID = 96
 C_IN = 18
 SLOTS = 256
-PAIRS = 6
-BANDS = 10
+PAIRS = 8
+BANDS = 14
 K_IN = 224
 NEIGHBOURS = ((0, -1), (0, 1), (-1, -1), (1, -1), (-1, 1), (1, 1), (-1, 0), (1, 0))
-SLOT_OF = (0, 1, 4, 5, 2, 3)
-ROWS_SENDS = tuple(
-    (dt, dr, slice(1, 2) if dr < 0 else slice(2, 3), slice(3, 4) if dr < 0 else slice(0, 1))
-    for dt, dr in NEIGHBOURS[:6]
+TOP, MID, BOTTOM = slice(1, 3), slice(3, 5), slice(5, 7)
+FIRST_SENDS = tuple(
+    (dt, dr, *{-1: (slice(2, 4), slice(6, 8)), 1: (slice(4, 6), slice(0, 2)), 0: (slice(2, 6), slice(2, 6))}[dr])
+    for dt, dr in NEIGHBOURS
 )
-EDGE_SENDS = tuple((dt, 0, slice(1, 3), slice(1, 3)) for dt in (-1, 1))
-MID_SENDS = tuple((dt, 0, slice(4, 6), slice(4, 6)) for dt in (-1, 1))
-SENDS = ROWS_SENDS + EDGE_SENDS + MID_SENDS
-INNER_BANDS = (4, 5, 2, 3, 6, 7)
-OUTER_BANDS = (0, 1, 8, 9)
+SECOND_SENDS = tuple((dt, 0, part, part) for part in (MID, TOP, BOTTOM) for dt in (-1, 1))
 
 
 def three_parts(values):
@@ -129,8 +125,8 @@
     obs_col,
     obs_value,
     state,
-    turned_first,
     turned_second,
+    affine,
     w1_turned,
     w1,
     w2,
@@ -161,14 +157,14 @@
         for i, (src, dst) in enumerate(
             (
                 (x_hbm, x_in),
-                (w1_hbm, w1_raw),
-                (embed_hbm, embed_raw),
-                (w2_hbm, w2_raw),
                 (step_hbm, obs_step),
                 (row_hbm, obs_row),
                 (col_hbm, obs_col),
                 (value_hbm, obs_value),
                 (first_hbm, first),
+                (w1_hbm, w1_raw),
+                (embed_hbm, embed_raw),
+                (w2_hbm, w2_raw),
                 (second_hbm, second),
             )
         )
@@ -176,8 +172,8 @@
     for load in loads:
         load.start()
 
-    copies = [
-        [
+    def copies_of(index, sends):
+        return [
             pltpu.make_async_remote_copy(
                 src_ref=tiles.at[index, 1, source],
                 dst_ref=tiles.at[index, 1 - dt, target],
@@ -186,18 +182,32 @@
                 device_id=peer(dt, dr),
                 device_id_type=MESH,
             )
-            for k, (dt, dr, source, target) in enumerate(SENDS)
+            for k, (dt, dr, source, target) in enumerate(sends)
         ]
-        for index in range(2)
+
+    first_copies = copies_of(0, FIRST_SENDS)
+    second_copies = copies_of(1, SECOND_SENDS)
+    affine_copies = [
+        pltpu.make_async_remote_copy(
+            src_ref=affine.at[source],
+            dst_ref=affine.at[target],
+            send_sem=send_sems.at[2, k],
+            recv_sem=recv_sems.at[2, k],
+            device_id=peer(0, dr),
+            device_id_type=MESH,
+        )
+        for k, (dr, source, target) in enumerate(
+            ((-1, slice(2, 4), slice(10, 12)), (1, slice(8, 10), slice(0, 2)))
+        )
     ]
 
     def put_tiles(index, pair, upper, lower):
         scale = 1.0 / (1.0 + LEVELS[index] ** 2) ** 0.5
         tile = jnp.concatenate([upper, lower], axis=0) * scale
-        tiles[index, 1, SLOT_OF[pair + 1]] = tile.astype(jnp.bfloat16)
+        tiles[index, 1, pair] = tile.astype(jnp.bfloat16)
 
     def unpack(index, pair, block):
-        tile = tiles[index, block, SLOT_OF[pair]].astype(jnp.float32)
+        tile = tiles[index, block, pair].astype(jnp.float32)
         if block == 0:
             tile = jnp.where(tm == 0, 0.0, tile)
         if block == 2:
@@ -215,92 +225,109 @@
         hidden = (half + half * jnp.tanh(half)).astype(jnp.bfloat16)
         taps[j] = jnp.dot(w2[...], hidden, preferred_element_type=jnp.float32)
 
-    def finish_row(index, r, noise):
+    def affine_row(index, r, current, noise):
         level_now, level_next = LEVELS[index], LEVELS[index + 1]
-        sums = []
-        for b in range(3):
-            at = b * 24
-            sums.append(
-                taps[r, at : at + 8, :] + taps[r + 1, at + 8 : at + 16, :] + taps[r + 2, at + 16 : at + 24, :]
-            )
-        net = sums[1] + pltpu.roll(sums[0], 1, 1) + pltpu.roll(sums[2], COLS - 1, 1)
-        current = state[r]
         base = 1.0 + level_now**2
-        denoised = current * (1.0 / base) + (level_now / base**0.5) * net
+        spread = level_now**2 - level_next**2
+        keep = 1.0 / level_now**2
+        gain = 1.0 / (OBS_NOISE + COVARIANCE_GAIN * level_now**2)
         hits = guide[r * 8 : r * 8 + 8, :]
         values = guide[64 + r * 8 : 64 + r * 8 + 8, :]
-        misfit = (values - hits * denoised) * (1.0 / (OBS_NOISE + COVARIANCE_GAIN * level_now**2))
-        score = (denoised - current) * (1.0 / level_now**2) + misfit
-        spread = level_now**2 - level_next**2
-        return current + spread * score + spread**0.5 * noise[r]
+        still = current * (1.0 / base)
+        score = (still - current) * keep + (values - hits * still) * gain
+        shift = current + spread * score + spread**0.5 * noise
+        slope = (spread * level_now / base**0.5) * (keep - gain * hits)
+        return shift, slope
+
+    def net_row(r):
+        at = r
+        sums = [
+            taps[at, b * 24 : b * 24 + 8, :]
+            + taps[at + 1, b * 24 + 8 : b * 24 + 16, :]
+            + taps[at + 2, b * 24 + 16 : b * 24 + 24, :]
+            for b in range(3)
+        ]
+        return sums[1] + pltpu.roll(sums[0], 1, 1) + pltpu.roll(sums[2], COLS - 1, 1)
 
     def step_pair(pair):
-        slabs = [finish_row(0, 2 * pair + half, turned_first) for half in range(2)]
+        slabs = []
+        for half in range(2):
+            r = 2 * (pair - 1) + half
+            slabs.append(affine[r, 0:8, :] + affine[r, 8:16, :] * net_row(r))
         put_tiles(1, pair, *slabs)
-        for half in range(2):
-            state[2 * pair + half] = slabs[half]
-
-    n_rows_sends = len(ROWS_SENDS)
-
-    def exchange_inner(index):
-        for pair in range(1, 5):
-            unpack(index, pair, 1)
-        for copy in copies[index][n_rows_sends:]:
-            copy.wait_recv()
-        for pair in range(1, 5):
-            unpack(index, pair, 0)
-            unpack(index, pair, 2)
-
-    def exchange_outer(index):
-        for copy in copies[index][:n_rows_sends]:
-            copy.wait_recv()
-        for block in range(3):
-            unpack(index, 0, block)
-            unpack(index, 5, block)
+        if 2 <= pair < 6:
+            for half in range(2):
+                state[2 * (pair - 2) + half] = slabs[half]
+
+    def unpack_pairs(index, pairs, blocks):
+        for pair in pairs:
+            for block in blocks:
+                unpack(index, pair, block)
+
+    def bands(index, rows):
+        for j in rows:
+            hidden_band(index, j)
 
     loads[0].wait()
     state[...] = jnp.swapaxes(x_in[...].reshape(TL, ROWS, COLS), 0, 1)
     for pair in range(4):
-        put_tiles(0, pair, state[2 * pair], state[2 * pair + 1])
-    for load in loads[1:4]:
+        put_tiles(0, pair + 2, state[2 * pair], state[2 * pair + 1])
+    for load in loads[1:6]:
+        load.wait()
+    build_guide(count, obs_step, obs_row, obs_col, obs_value, guide)
+    turned = jnp.swapaxes(first[...].reshape(TL, ROWS, COLS), 0, 1)
+    for r in range(ROWS):
+        shift, slope = affine_row(0, r, state[r], turned[r])
+        affine[r + 2, 0:8, :] = shift
+        affine[r + 2, 8:16, :] = slope
+    pl.semaphore_wait(barrier, len(NEIGHBOURS))
+    for copy in first_copies:
+        copy.start()
+    for copy in affine_copies:
+        copy.start()
+    for load in loads[6:]:
         load.wait()
     build_conv_in(w1_raw, embed_raw, w1_turned, w1)
     build_conv_out(w2_raw, w2)
-    pl.semaphore_wait(barrier, len(NEIGHBOURS))
-    for copy in copies[0]:
+    turned_second[...] = jnp.swapaxes(second[...].reshape(TL, ROWS, COLS), 0, 1)
+
+    unpack_pairs(0, range(2, 6), (1,))
+    for copy in first_copies[6:]:
+        copy.wait_recv()
+    unpack_pairs(0, range(2, 6), (0, 2))
+    bands(0, range(4, 10))
+    for pair in (3, 4):
+        step_pair(pair)
+    for copy in second_copies[:2]:
         copy.start()
-    for load in loads[4:]:
-        load.wait()
-    build_guide(count, obs_step, obs_row, obs_col, obs_value, guide)
-    turned_first[...] = jnp.swapaxes(first[...].reshape(TL, ROWS, COLS), 0, 1)
-    turned_second[...] = jnp.swapaxes(second[...].reshape(TL, ROWS, COLS), 0, 1)
-
-    exchange_inner(0)
-    for j in INNER_BANDS:
-        hidden_band(0, j)
+    for copy in first_copies[:6]:
+        copy.wait_recv()
+    unpack_pairs(0, (0, 1, 6, 7), range(3))
+    for copy in affine_copies:
+        copy.wait_recv()
+    bands(0, range(0, 4))
     for pair in (1, 2):
         step_pair(pair)
-    for copy in copies[1][n_rows_sends + 2 :]:
+    for copy in second_copies[2:4]:
         copy.start()
-    exchange_outer(0)
-    for j in OUTER_BANDS:
-        hidden_band(0, j)
-    for pair in (0, 3):
+    bands(0, range(10, 14))
+    for pair in (5, 6):
         step_pair(pair)
-    for copy in copies[1][: n_rows_sends + 2]:
+    for copy in second_copies[4:]:
         copy.start()
 
-    exchange_inner(1)
-    for j in INNER_BANDS:
-        hidden_band(1, j)
-    exchange_outer(1)
-    for j in OUTER_BANDS:
-        hidden_band(1, j)
-    done = jnp.stack([finish_row(1, r, turned_second) for r in range(ROWS)], axis=0)
-    out[...] = jnp.swapaxes(done, 0, 1).reshape(TL * ROWS, COLS)
-    for index in range(2):
-        for copy in copies[index]:
-            copy.wait_send()
+    unpack_pairs(1, range(1, 7), (1,))
+    for copy in second_copies:
+        copy.wait_recv()
+    unpack_pairs(1, range(1, 7), (0, 2))
+    bands(1, range(2, 12))
+    done = []
+    for r in range(ROWS):
+        shift, slope = affine_row(1, r, state[r], turned_second[r])
+        done.append(shift + slope * net_row(r + 2))
+    out[...] = jnp.swapaxes(jnp.stack(done, axis=0), 0, 1).reshape(TL * ROWS, COLS)
+    for copy in (*first_copies, *affine_copies, *second_copies):
+        copy.wait_send()
 
 
 def per_device(
@@ -338,7 +365,7 @@
             pltpu.VMEM(slots, jnp.float32),
             pltpu.VMEM((ROWS, TL, COLS), jnp.float32),
             pltpu.VMEM((ROWS, TL, COLS), jnp.float32),
-            pltpu.VMEM((ROWS, TL, COLS), jnp.float32),
+            pltpu.VMEM((ROWS + 4, 2 * TL, COLS), jnp.float32),
             pltpu.VMEM((256, 128), jnp.float32),
             pltpu.VMEM((T * HID, K_IN), jnp.bfloat16),
             pltpu.VMEM((72, T * HID), jnp.bfloat16),
@@ -347,8 +374,8 @@
             pltpu.VMEM((2 * PAIRS * 72, COLS), jnp.float32),
             pltpu.VMEM((BANDS, 72, COLS), jnp.float32),
             pltpu.SemaphoreType.DMA((10,)),
-            pltpu.SemaphoreType.DMA((2, len(SENDS))),
-            pltpu.SemaphoreType.DMA((2, len(SENDS))),
+            pltpu.SemaphoreType.DMA((3, len(NEIGHBOURS))),
+            pltpu.SemaphoreType.DMA((3, len(NEIGHBOURS))),
         ],
         compiler_params=pltpu.CompilerParams(
             collective_id=0, has_side_effects=True, vmem_limit_bytes=32 * 1024 * 1024

time: 27.6 us -> 31 us (1.12)
  the two profiles are of different devices: /device:TPU:1 before, /device:TPU:16 now
where the time goes in v3:
time: 31 us; the launch traced here: 30.9 us
  Pallas kernels  29.6 us (95%)
  between operations  0.66 us (2%)
  local copies, waits for them, and re-layouts  0.63 us (2%)
    pallas_call x1, Pallas kernels, per_device(): pl.pallas_call(functools.partial(kernel, sizes), out_shape=pltpu.VMEM(fla...  29.6 us
    unnamed x1, local copies, waits for them, and re-layouts  0.63 us

profile of v3, /device:TPU:16, one launch (start us, length us, event | category | flops | bytes accessed | tf_op | source)
XLA Modules:
  0.0 30.9 jit_solution(6904633144682447790)
XLA Ops:
  0.7 29.6 %reverse_steps.1 = f32[64,256]{1,0:T(8,128)S(1)} custom-call(f32[64,256]{1,0:T(8,128)} %bitcast.11, f32[64,256]{1,0:T(8,128)} %bitcast.12, f32[64,256]{1,0:T(8,128)} %bitcast.13, bf16[9,18,96]{2,1,0:T(8,128)(2,1)} %bitcast.14, bf16[9,2,96]{2,1,0:T(2,128)(2,1)} %w2_hbm.1, f32[1,96]{1,0:T(1,128)} %bitcast.19, s32[1,1]{1,0:T(1,128)S(6)} %copy.14.count, ...), custom_call_target="tpu_custom_call" | custom-call | tf_op jit(solution)/shard_map/reverse_steps/pallas_call | solution.py:350
  30.3 0.6 %copy.13 = f32[4,2,8,256]{3,2,1,0:T(8,128)} copy(f32[4,2,8,256]{3,2,1,0:T(8,128)S(1)} %bitcast.10) | data formatting | bytes 131072

commit v4 on v2

--- a/solution.py
+++ b/solution.py
@@ -208,12 +208,20 @@
                 at = (2 * pair + half) * 72 + b * 24 + block * 8
                 frames[at : at + 8, :] = moved[half * 8 : half * 8 + 8]
 
-    def hidden_band(index, j):
+    def hidden_bands(index, group):
         ones = jnp.full((K_IN - 216, COLS), LEVELS[index], jnp.float32)
-        window = jnp.concatenate([frames[72 * j : 72 * j + 216, :], ones], axis=0).astype(jnp.bfloat16)
-        half = jnp.dot(w1[...], window, preferred_element_type=jnp.float32)
+        windows = jnp.concatenate(
+            [
+                jnp.concatenate([frames[72 * j : 72 * j + 216, :], ones], axis=0).astype(jnp.bfloat16)
+                for j in group
+            ],
+            axis=1,
+        )
+        half = jnp.dot(w1[...], windows, preferred_element_type=jnp.float32)
         hidden = (half + half * jnp.tanh(half)).astype(jnp.bfloat16)
-        taps[j] = jnp.dot(w2[...], hidden, preferred_element_type=jnp.float32)
+        found = jnp.dot(w2[...], hidden, preferred_element_type=jnp.float32)
+        for k, j in enumerate(group):
+            taps[j] = found[:, k * COLS : (k + 1) * COLS]
 
     def finish_row(index, r, noise):
         level_now, level_next = LEVELS[index], LEVELS[index + 1]
@@ -276,26 +284,26 @@
     turned_second[...] = jnp.swapaxes(second[...].reshape(TL, ROWS, COLS), 0, 1)
 
     exchange_inner(0)
-    for j in INNER_BANDS:
-        hidden_band(0, j)
+    for at in range(0, len(INNER_BANDS), 6):
+        hidden_bands(0, INNER_BANDS[at : at + 6])
     for pair in (1, 2):
         step_pair(pair)
     for copy in copies[1][n_rows_sends + 2 :]:
         copy.start()
     exchange_outer(0)
-    for j in OUTER_BANDS:
-        hidden_band(0, j)
+    for at in range(0, len(OUTER_BANDS), 6):
+        hidden_bands(0, OUTER_BANDS[at : at + 6])
     for pair in (0, 3):
         step_pair(pair)
     for copy in copies[1][: n_rows_sends + 2]:
         copy.start()
 
     exchange_inner(1)
-    for j in INNER_BANDS:
-        hidden_band(1, j)
+    for at in range(0, len(INNER_BANDS), 6):
+        hidden_bands(1, INNER_BANDS[at : at + 6])
     exchange_outer(1)
-    for j in OUTER_BANDS:
-        hidden_band(1, j)
+    for at in range(0, len(OUTER_BANDS), 6):
+        hidden_bands(1, OUTER_BANDS[at : at + 6])
     done = jnp.stack([finish_row(1, r, turned_second) for r in range(ROWS)], axis=0)
     out[...] = jnp.swapaxes(done, 0, 1).reshape(TL * ROWS, COLS)
     for index in range(2):

time: 27.6 us -> 26.1 us (0.946)
  Pallas kernels: 26.2 us -> 24.7 us
    pallas_call x1, Pallas kernels: 26.2 us -> 24.7 us  [per_device(): pl.pallas_call(functools.partial(kernel, sizes), out_shape=pltpu.VMEM(fla...]
where the time goes in v4:
time: 26.1 us; the launch traced here: 25.9 us
  Pallas kernels  24.7 us (95%)
  between operations  0.66 us (3%)
  local copies, waits for them, and re-layouts  0.63 us (2%)
    pallas_call x1, Pallas kernels, per_device(): pl.pallas_call(functools.partial(kernel, sizes), out_shape=pltpu.VMEM(fla...  24.7 us
    unnamed x1, local copies, waits for them, and re-layouts  0.63 us

profile of v4, /device:TPU:1, one launch (start us, length us, event | category | flops | bytes accessed | tf_op | source)
XLA Modules:
  0.0 25.9 jit_solution(9914410764000582169)
XLA Ops:
  0.7 24.7 %reverse_steps.1 = f32[64,256]{1,0:T(8,128)S(1)} custom-call(f32[64,256]{1,0:T(8,128)} %bitcast.11, f32[64,256]{1,0:T(8,128)} %bitcast.12, f32[64,256]{1,0:T(8,128)} %bitcast.13, bf16[9,18,96]{2,1,0:T(8,128)(2,1)} %bitcast.14, bf16[9,2,96]{2,1,0:T(2,128)(2,1)} %w2_hbm.1, f32[1,96]{1,0:T(1,128)} %bitcast.19, s32[1,1]{1,0:T(1,128)S(6)} %copy.14.count, ...), custom_call_target="tpu_custom_call" | custom-call | tf_op jit(solution)/shard_map/reverse_steps/pallas_call | solution.py:331
  25.3 0.6 %copy.13 = f32[4,2,8,256]{3,2,1,0:T(8,128)} copy(f32[4,2,8,256]{3,2,1,0:T(8,128)S(1)} %bitcast.10) | data formatting | bytes 131072

commit v5 on v4

--- a/solution.py
+++ b/solution.py
@@ -24,15 +24,8 @@
 K_IN = 224
 NEIGHBOURS = ((0, -1), (0, 1), (-1, -1), (1, -1), (-1, 1), (1, 1), (-1, 0), (1, 0))
 SLOT_OF = (0, 1, 4, 5, 2, 3)
-ROWS_SENDS = tuple(
-    (dt, dr, slice(1, 2) if dr < 0 else slice(2, 3), slice(3, 4) if dr < 0 else slice(0, 1))
-    for dt, dr in NEIGHBOURS[:6]
-)
-EDGE_SENDS = tuple((dt, 0, slice(1, 3), slice(1, 3)) for dt in (-1, 1))
-MID_SENDS = tuple((dt, 0, slice(4, 6), slice(4, 6)) for dt in (-1, 1))
-SENDS = ROWS_SENDS + EDGE_SENDS + MID_SENDS
+FAR, NEAR, EDGES, MIDS = slice(0, 3), slice(3, 6), slice(6, 8), slice(8, 10)
 INNER_BANDS = (4, 5, 2, 3, 6, 7)
-OUTER_BANDS = (0, 1, 8, 9)
 
 
 def three_parts(values):
@@ -129,8 +122,8 @@
     obs_col,
     obs_value,
     state,
-    turned_first,
-    turned_second,
+    shift,
+    slope,
     w1_turned,
     w1,
     w2,
@@ -176,28 +169,40 @@
     for load in loads:
         load.start()
 
-    copies = [
-        [
-            pltpu.make_async_remote_copy(
-                src_ref=tiles.at[index, 1, source],
-                dst_ref=tiles.at[index, 1 - dt, target],
-                send_sem=send_sems.at[index, k],
-                recv_sem=recv_sems.at[index, k],
-                device_id=peer(dt, dr),
-                device_id_type=MESH,
-            )
-            for k, (dt, dr, source, target) in enumerate(SENDS)
-        ]
-        for index in range(2)
-    ]
-
-    def put_tiles(index, pair, upper, lower):
+    far_side = lax.rem(rw, 2)
+    near_side = 1 - far_side
+
+    def copy_to(index, k, dt, rows_to, source, target):
+        return pltpu.make_async_remote_copy(
+            src_ref=tiles.at[index, 1, source],
+            dst_ref=tiles.at[index, 1 - dt, target],
+            send_sem=send_sems.at[index, k],
+            recv_sem=recv_sems.at[index, k],
+            device_id={"tm": peer(dt, 0)["tm"], "rows": rows_to},
+            device_id_type=MESH,
+        )
+
+    copies = []
+    for index in range(2):
+        made = []
+        for side in (far_side, near_side):
+            rows_to = lax.rem(rw + 2 * side - 1 + n_rows, n_rows)
+            for dt in (-1, 1, 0):
+                made.append(
+                    copy_to(index, len(made), dt, rows_to, pl.ds(1 + side, 1), pl.ds(3 - 3 * side, 1))
+                )
+        for part in (slice(1, 3), slice(4, 6)):
+            for dt in (-1, 1):
+                made.append(copy_to(index, len(made), dt, rw, part, part))
+        copies.append(made)
+
+    def put_tiles(index, slot, upper, lower):
         scale = 1.0 / (1.0 + LEVELS[index] ** 2) ** 0.5
         tile = jnp.concatenate([upper, lower], axis=0) * scale
-        tiles[index, 1, SLOT_OF[pair + 1]] = tile.astype(jnp.bfloat16)
-
-    def unpack(index, pair, block):
-        tile = tiles[index, block, SLOT_OF[pair]].astype(jnp.float32)
+        tiles[index, 1, slot] = tile.astype(jnp.bfloat16)
+
+    def unpack(index, slot, at_row, block):
+        tile = tiles[index, block, slot].astype(jnp.float32)
         if block == 0:
             tile = jnp.where(tm == 0, 0.0, tile)
         if block == 2:
@@ -205,14 +210,16 @@
         for b in range(3):
             moved = pltpu.roll(tile, (1 - b) % COLS, 1) if b != 1 else tile
             for half in range(2):
-                at = (2 * pair + half) * 72 + b * 24 + block * 8
-                frames[at : at + 8, :] = moved[half * 8 : half * 8 + 8]
+                at = pl.multiple_of((at_row + half) * 72 + b * 24 + block * 8, 8)
+                frames[pl.ds(at, 8), :] = moved[half * 8 : half * 8 + 8]
 
     def hidden_bands(index, group):
         ones = jnp.full((K_IN - 216, COLS), LEVELS[index], jnp.float32)
         windows = jnp.concatenate(
             [
-                jnp.concatenate([frames[72 * j : 72 * j + 216, :], ones], axis=0).astype(jnp.bfloat16)
+                jnp.concatenate([frames[pl.ds(pl.multiple_of(72 * j, 8), 216), :], ones], axis=0).astype(
+                    jnp.bfloat16
+                )
                 for j in group
             ],
             axis=1,
@@ -223,89 +230,92 @@
         for k, j in enumerate(group):
             taps[j] = found[:, k * COLS : (k + 1) * COLS]
 
-    def finish_row(index, r, noise):
+    def prepare_rows(index, noise):
         level_now, level_next = LEVELS[index], LEVELS[index + 1]
-        sums = []
-        for b in range(3):
-            at = b * 24
-            sums.append(
-                taps[r, at : at + 8, :] + taps[r + 1, at + 8 : at + 16, :] + taps[r + 2, at + 16 : at + 24, :]
-            )
+        base = 1.0 + level_now**2
+        spread = level_now**2 - level_next**2
+        keep = 1.0 / level_now**2
+        gain = 1.0 / (OBS_NOISE + COVARIANCE_GAIN * level_now**2)
+        turned = jnp.swapaxes(noise[...].reshape(TL, ROWS, COLS), 0, 1)
+        for r in range(ROWS):
+            current = state[r]
+            hits = guide[r * 8 : r * 8 + 8, :]
+            values = guide[64 + r * 8 : 64 + r * 8 + 8, :]
+            still = current * (1.0 / base)
+            score = (still - current) * keep + (values - hits * still) * gain
+            shift[r] = current + spread * score + spread**0.5 * turned[r]
+            slope[r] = (spread * level_now / base**0.5) * (keep - gain * hits)
+
+    def finish_row(r):
+        sums = [
+            taps[r, b * 24 : b * 24 + 8, :]
+            + taps[r + 1, b * 24 + 8 : b * 24 + 16, :]
+            + taps[r + 2, b * 24 + 16 : b * 24 + 24, :]
+            for b in range(3)
+        ]
         net = sums[1] + pltpu.roll(sums[0], 1, 1) + pltpu.roll(sums[2], COLS - 1, 1)
-        current = state[r]
-        base = 1.0 + level_now**2
-        denoised = current * (1.0 / base) + (level_now / base**0.5) * net
-        hits = guide[r * 8 : r * 8 + 8, :]
-        values = guide[64 + r * 8 : 64 + r * 8 + 8, :]
-        misfit = (values - hits * denoised) * (1.0 / (OBS_NOISE + COVARIANCE_GAIN * level_now**2))
-        score = (denoised - current) * (1.0 / level_now**2) + misfit
-        spread = level_now**2 - level_next**2
-        return current + spread * score + spread**0.5 * noise[r]
-
-    def step_pair(pair):
-        slabs = [finish_row(0, 2 * pair + half, turned_first) for half in range(2)]
-        put_tiles(1, pair, *slabs)
-        for half in range(2):
-            state[2 * pair + half] = slabs[half]
-
-    n_rows_sends = len(ROWS_SENDS)
+        slab = shift[r] + slope[r] * net
+        state[r] = slab
+        return slab
+
+    def finish_pair(index, pair, slot):
+        slabs = [finish_row(2 * pair + half) for half in range(2)]
+        if index == 0:
+            put_tiles(1, slot, *slabs)
 
     def exchange_inner(index):
         for pair in range(1, 5):
-            unpack(index, pair, 1)
-        for copy in copies[index][n_rows_sends:]:
-            copy.wait_recv()
+            unpack(index, SLOT_OF[pair], 2 * pair, 1)
+        for part in (EDGES, MIDS):
+            for copy in copies[index][part]:
+                copy.wait_recv()
         for pair in range(1, 5):
-            unpack(index, pair, 0)
-            unpack(index, pair, 2)
-
-    def exchange_outer(index):
-        for copy in copies[index][:n_rows_sends]:
+            unpack(index, SLOT_OF[pair], 2 * pair, 0)
+            unpack(index, SLOT_OF[pair], 2 * pair, 2)
+        hidden_bands(index, INNER_BANDS)
+        for pair in (1, 2):
+            finish_pair(index, pair, SLOT_OF[pair + 1])
+
+    def exchange_outer(index, side, part):
+        for copy in copies[index][part]:
             copy.wait_recv()
         for block in range(3):
-            unpack(index, 0, block)
-            unpack(index, 5, block)
+            unpack(index, 3 * side, 10 * side, block)
+        hidden_bands(index, (8 * side, 8 * side + 1))
+        finish_pair(index, 3 * side, 1 + side)
+
+    def start(index, part):
+        for copy in copies[index][part]:
+            copy.start()
 
     loads[0].wait()
     state[...] = jnp.swapaxes(x_in[...].reshape(TL, ROWS, COLS), 0, 1)
     for pair in range(4):
-        put_tiles(0, pair, state[2 * pair], state[2 * pair + 1])
+        put_tiles(0, SLOT_OF[pair + 1], state[2 * pair], state[2 * pair + 1])
     for load in loads[1:4]:
         load.wait()
     build_conv_in(w1_raw, embed_raw, w1_turned, w1)
     build_conv_out(w2_raw, w2)
     pl.semaphore_wait(barrier, len(NEIGHBOURS))
-    for copy in copies[0]:
-        copy.start()
+    for part in (FAR, NEAR, EDGES, MIDS):
+        start(0, part)
     for load in loads[4:]:
         load.wait()
     build_guide(count, obs_step, obs_row, obs_col, obs_value, guide)
-    turned_first[...] = jnp.swapaxes(first[...].reshape(TL, ROWS, COLS), 0, 1)
-    turned_second[...] = jnp.swapaxes(second[...].reshape(TL, ROWS, COLS), 0, 1)
+    prepare_rows(0, first)
 
     exchange_inner(0)
-    for at in range(0, len(INNER_BANDS), 6):
-        hidden_bands(0, INNER_BANDS[at : at + 6])
-    for pair in (1, 2):
-        step_pair(pair)
-    for copy in copies[1][n_rows_sends + 2 :]:
-        copy.start()
-    exchange_outer(0)
-    for at in range(0, len(OUTER_BANDS), 6):
-        hidden_bands(0, OUTER_BANDS[at : at + 6])
-    for pair in (0, 3):
-        step_pair(pair)
-    for copy in copies[1][: n_rows_sends + 2]:
-        copy.start()
-
+    start(1, MIDS)
+    exchange_outer(0, near_side, NEAR)
+    start(1, NEAR)
+    exchange_outer(0, far_side, FAR)
+    start(1, FAR)
+    start(1, EDGES)
+    prepare_rows(1, second)
     exchange_inner(1)
-    for at in range(0, len(INNER_BANDS), 6):
-        hidden_bands(1, INNER_BANDS[at : at + 6])
-    exchange_outer(1)
-    for at in range(0, len(OUTER_BANDS), 6):
-        hidden_bands(1, OUTER_BANDS[at : at + 6])
-    done = jnp.stack([finish_row(1, r, turned_second) for r in range(ROWS)], axis=0)
-    out[...] = jnp.swapaxes(done, 0, 1).reshape(TL * ROWS, COLS)
+    exchange_outer(1, near_side, NEAR)
+    exchange_outer(1, far_side, FAR)
+    out[...] = jnp.swapaxes(state[...], 0, 1).reshape(TL * ROWS, COLS)
     for index in range(2):
         for copy in copies[index]:
             copy.wait_send()
@@ -355,8 +365,8 @@
             pltpu.VMEM((2 * PAIRS * 72, COLS), jnp.float32),
             pltpu.VMEM((BANDS, 72, COLS), jnp.float32),
             pltpu.SemaphoreType.DMA((10,)),
-            pltpu.SemaphoreType.DMA((2, len(SENDS))),
-            pltpu.SemaphoreType.DMA((2, len(SENDS))),
+            pltpu.SemaphoreType.DMA((2, 10)),
+            pltpu.SemaphoreType.DMA((2, 10)),
         ],
         compiler_params=pltpu.CompilerParams(
             collective_id=0, has_side_effects=True, vmem_limit_bytes=32 * 1024 * 1024

time: 26.1 us -> 25.5 us (0.977)
  Pallas kernels: 24.7 us -> 24 us
    pallas_call x1, Pallas kernels: 24.7 us -> 24 us  [per_device(): pl.pallas_call(functools.partial(kernel, sizes), out_shape=pltpu.VMEM(fla...]
where the time goes in v5:
time: 25.5 us; the launch traced here: 25.3 us
  Pallas kernels  24 us (94%)
  between operations  0.66 us (3%)
  local copies, waits for them, and re-layouts  0.63 us (2%)
    pallas_call x1, Pallas kernels, per_device(): pl.pallas_call(functools.partial(kernel, sizes), out_shape=pltpu.VMEM(fla...  24 us
    unnamed x1, local copies, waits for them, and re-layouts  0.63 us

profile of v5, /device:TPU:1, one launch (start us, length us, event | category | flops | bytes accessed | tf_op | source)
XLA Modules:
  0.0 25.3 jit_solution(259620467450661769)
XLA Ops:
  0.7 24.0 %reverse_steps.1 = f32[64,256]{1,0:T(8,128)S(1)} custom-call(f32[64,256]{1,0:T(8,128)} %bitcast.11, f32[64,256]{1,0:T(8,128)} %bitcast.12, f32[64,256]{1,0:T(8,128)} %bitcast.13, bf16[9,18,96]{2,1,0:T(8,128)(2,1)} %bitcast.14, bf16[9,2,96]{2,1,0:T(2,128)(2,1)} %w2_hbm.1, f32[1,96]{1,0:T(1,128)} %bitcast.19, s32[1,1]{1,0:T(1,128)S(6)} %copy.14.count, ...), custom_call_target="tpu_custom_call" | custom-call | tf_op jit(solution)/shard_map/reverse_steps/pallas_call | solution.py:341
  24.7 0.6 %copy.13 = f32[4,2,8,256]{3,2,1,0:T(8,128)} copy(f32[4,2,8,256]{3,2,1,0:T(8,128)S(1)} %bitcast.10) | data formatting | bytes 131072

commit v6 on v5

--- a/solution.py
+++ b/solution.py
@@ -292,15 +292,15 @@
     state[...] = jnp.swapaxes(x_in[...].reshape(TL, ROWS, COLS), 0, 1)
     for pair in range(4):
         put_tiles(0, SLOT_OF[pair + 1], state[2 * pair], state[2 * pair + 1])
-    for load in loads[1:4]:
+    pl.semaphore_wait(barrier, len(NEIGHBOURS))
+    start(0, FAR)
+    for load in loads[1:]:
         load.wait()
+    start(0, NEAR)
     build_conv_in(w1_raw, embed_raw, w1_turned, w1)
+    start(0, EDGES)
+    start(0, MIDS)
     build_conv_out(w2_raw, w2)
-    pl.semaphore_wait(barrier, len(NEIGHBOURS))
-    for part in (FAR, NEAR, EDGES, MIDS):
-        start(0, part)
-    for load in loads[4:]:
-        load.wait()
     build_guide(count, obs_step, obs_row, obs_col, obs_value, guide)
     prepare_rows(0, first)
 
@@ -314,11 +314,11 @@
     prepare_rows(1, second)
     exchange_inner(1)
     exchange_outer(1, near_side, NEAR)
-    exchange_outer(1, far_side, FAR)
-    out[...] = jnp.swapaxes(state[...], 0, 1).reshape(TL * ROWS, COLS)
     for index in range(2):
         for copy in copies[index]:
             copy.wait_send()
+    exchange_outer(1, far_side, FAR)
+    out[...] = jnp.swapaxes(state[...], 0, 1).reshape(TL * ROWS, COLS)
 
 
 def per_device(

time: 25.5 us -> 25.4 us (level)
  no operation moved by 1% of the time
where the time goes in v6:
time: 25.4 us; the launch traced here: 25.3 us
  Pallas kernels  24 us (94%)
  between operations  0.66 us (3%)
  local copies, waits for them, and re-layouts  0.63 us (2%)
    pallas_call x1, Pallas kernels, per_device(): pl.pallas_call(functools.partial(kernel, sizes), out_shape=pltpu.VMEM(fla...  24 us
    unnamed x1, local copies, waits for them, and re-layouts  0.63 us

profile of v6, /device:TPU:1, one launch (start us, length us, event | category | flops | bytes accessed | tf_op | source)
XLA Modules:
  0.0 25.3 jit_solution(10924906498799588393)
XLA Ops:
  0.7 24.0 %reverse_steps.1 = f32[64,256]{1,0:T(8,128)S(1)} custom-call(f32[64,256]{1,0:T(8,128)} %bitcast.11, f32[64,256]{1,0:T(8,128)} %bitcast.12, f32[64,256]{1,0:T(8,128)} %bitcast.13, bf16[9,18,96]{2,1,0:T(8,128)(2,1)} %bitcast.14, bf16[9,2,96]{2,1,0:T(2,128)(2,1)} %w2_hbm.1, f32[1,96]{1,0:T(1,128)} %bitcast.19, s32[1,1]{1,0:T(1,128)S(6)} %copy.14.count, ...), custom_call_target="tpu_custom_call" | custom-call | tf_op jit(solution)/shard_map/reverse_steps/pallas_call | solution.py:341
  24.7 0.6 %copy.13 = f32[4,2,8,256]{3,2,1,0:T(8,128)} copy(f32[4,2,8,256]{3,2,1,0:T(8,128)S(1)} %bitcast.10) | data formatting | bytes 131072

commit v7 on v6

--- a/solution.py
+++ b/solution.py
@@ -310,8 +310,8 @@
     start(1, NEAR)
     exchange_outer(0, far_side, FAR)
     start(1, FAR)
+    prepare_rows(1, second)
     start(1, EDGES)
-    prepare_rows(1, second)
     exchange_inner(1)
     exchange_outer(1, near_side, NEAR)
     for index in range(2):

time: 25.4 us -> 25.4 us (level)
  no operation moved by 1% of the time
where the time goes in v7:
time: 25.4 us; the launch traced here: 25.3 us
  Pallas kernels  24 us (94%)
  between operations  0.66 us (3%)
  local copies, waits for them, and re-layouts  0.63 us (2%)
    pallas_call x1, Pallas kernels, per_device(): pl.pallas_call(functools.partial(kernel, sizes), out_shape=pltpu.VMEM(fla...  24 us
    unnamed x1, local copies, waits for them, and re-layouts  0.63 us

profile of v7, /device:TPU:1, one launch (start us, length us, event | category | flops | bytes accessed | tf_op | source)
XLA Modules:
  0.0 25.3 jit_solution(1779766467402808111)
XLA Ops:
  0.7 24.0 %reverse_steps.1 = f32[64,256]{1,0:T(8,128)S(1)} custom-call(f32[64,256]{1,0:T(8,128)} %bitcast.11, f32[64,256]{1,0:T(8,128)} %bitcast.12, f32[64,256]{1,0:T(8,128)} %bitcast.13, bf16[9,18,96]{2,1,0:T(8,128)(2,1)} %bitcast.14, bf16[9,2,96]{2,1,0:T(2,128)(2,1)} %w2_hbm.1, f32[1,96]{1,0:T(1,128)} %bitcast.19, s32[1,1]{1,0:T(1,128)S(6)} %copy.14.count, ...), custom_call_target="tpu_custom_call" | custom-call | tf_op jit(solution)/shard_map/reverse_steps/pallas_call | solution.py:341
  24.7 0.6 %copy.13 = f32[4,2,8,256]{3,2,1,0:T(8,128)} copy(f32[4,2,8,256]{3,2,1,0:T(8,128)S(1)} %bitcast.10) | data formatting | bytes 131072

commit v8 on v6

--- a/solution.py
+++ b/solution.py
@@ -146,8 +146,17 @@
         }
 
     barrier = pltpu.get_barrier_semaphore()
-    for dt, dr in NEIGHBOURS:
-        pl.semaphore_signal(barrier, inc=1, device_id=peer(dt, dr), device_id_type=MESH)
+    far_to = lax.rem(rw + 2 * lax.rem(rw, 2) - 1 + n_rows, n_rows)
+    near_to = lax.rem(rw + 1 - 2 * lax.rem(rw, 2) + n_rows, n_rows)
+    for rows_to in (far_to, near_to, rw):
+        for dt in (0, -1, 1):
+            if dt or rows_to is not rw:
+                pl.semaphore_signal(
+                    barrier,
+                    inc=1,
+                    device_id={"tm": peer(dt, 0)["tm"], "rows": rows_to},
+                    device_id_type=MESH,
+                )
 
     loads = [
         pltpu.make_async_copy(src, dst, load_sems.at[i])

time: 25.4 us -> 25.4 us (level)
  no operation moved by 1% of the time
where the time goes in v8:
time: 25.4 us; the launch traced here: 25.3 us
  Pallas kernels  24 us (94%)
  between operations  0.66 us (3%)
  local copies, waits for them, and re-layouts  0.63 us (2%)
    pallas_call x1, Pallas kernels, per_device(): pl.pallas_call(functools.partial(kernel, sizes), out_shape=pltpu.VMEM(fla...  24 us
    unnamed x1, local copies, waits for them, and re-layouts  0.63 us

profile of v8, /device:TPU:1, one launch (start us, length us, event | category | flops | bytes accessed | tf_op | source)
XLA Modules:
  0.0 25.3 jit_solution(7810549799369465672)
XLA Ops:
  0.7 24.0 %reverse_steps.1 = f32[64,256]{1,0:T(8,128)S(1)} custom-call(f32[64,256]{1,0:T(8,128)} %bitcast.11, f32[64,256]{1,0:T(8,128)} %bitcast.12, f32[64,256]{1,0:T(8,128)} %bitcast.13, bf16[9,18,96]{2,1,0:T(8,128)(2,1)} %bitcast.14, bf16[9,2,96]{2,1,0:T(2,128)(2,1)} %w2_hbm.1, f32[1,96]{1,0:T(1,128)} %bitcast.19, s32[1,1]{1,0:T(1,128)S(6)} %copy.14.count, ...), custom_call_target="tpu_custom_call" | custom-call | tf_op jit(solution)/shard_map/reverse_steps/pallas_call | solution.py:350
  24.7 0.6 %copy.13 = f32[4,2,8,256]{3,2,1,0:T(8,128)} copy(f32[4,2,8,256]{3,2,1,0:T(8,128)S(1)} %bitcast.10) | data formatting | bytes 131072
